TPU v7x, 32 devices: a whole 2x2x4 slice. The times are simulated.
32 devices in a mesh: dp: 8 (over y, x, core), fsdp: 4 (over z).
Axes of the slice: x: 2, y: 2, z: 4, core: 2. Of those that a mesh axis runs over, the one named last changes fastest.
Arguments:
- tokens: bfloat16 [4096, 2560], P(('dp', 'fsdp')), may hold values from -6 to 6
- cotangent: bfloat16 [4096, 2560], P(('dp', 'fsdp')), may hold values from -6 to 6
- seq_lengths: int32 [32, 2], P(('dp', 'fsdp')), may hold values from 0 to 128, as said below
- wq_master: float32 [2560, 2560], P('dp', 'fsdp'), may hold values from -0.125 to 0.125
- wkv_master: float32 [2560, 512], P('dp', 'fsdp'), may hold values from -0.125 to 0.125
- wo_master: float32 [2560, 2560], P('dp', 'fsdp'), may hold values from -0.625 to 0.625
- ffw_up_master: float32 [2, 2560, 7680], P(None, 'dp', 'fsdp'), may hold values from -0.125 to 0.125
- ffw_down_master: float32 [7680, 2560], P('fsdp', 'dp'), may hold values from -0.0625 to 0.0625
- vec_master: float32 [4, 2560], P(None, ('dp', 'fsdp')), may hold values from -1.5 to 2.6
- wq_first: float32 [2560, 2560], P('dp', 'fsdp'), may hold values from -1 to 1
- wq_second: float32 [2560, 2560], P('dp', 'fsdp'), may hold values from 0 to 1
- wkv_first: float32 [2560, 512], P('dp', 'fsdp'), may hold values from -1 to 1
- wkv_second: float32 [2560, 512], P('dp', 'fsdp'), may hold values from 0 to 1
- wo_first: float32 [2560, 2560], P('dp', 'fsdp'), may hold values from -1 to 1
- wo_second: float32 [2560, 2560], P('dp', 'fsdp'), may hold values from 0 to 1
- ffw_up_first: float32 [2, 2560, 7680], P(None, 'dp', 'fsdp'), may hold values from -1 to 1
- ffw_up_second: float32 [2, 2560, 7680], P(None, 'dp', 'fsdp'), may hold values from 0 to 1
- ffw_down_first: float32 [7680, 2560], P('fsdp', 'dp'), may hold values from -1 to 1
- ffw_down_second: float32 [7680, 2560], P('fsdp', 'dp'), may hold values from 0 to 1
- vec_first: float32 [4, 2560], P(None, ('dp', 'fsdp')), may hold values from -1 to 1
- vec_second: float32 [4, 2560], P(None, ('dp', 'fsdp')), may hold values from 0 to 1
Outputs:
- block_out: bfloat16 [4096, 2560], P(('dp', 'fsdp'))
- input_grad: bfloat16 [4096, 2560], P(('dp', 'fsdp'))
- grad_norm: float32 [], replicated
- wq_clipped: float32 [2560, 2560], P('dp', 'fsdp')
- wq_first_new: float32 [2560, 2560], P('dp', 'fsdp')
- wq_second_new: float32 [2560, 2560], P('dp', 'fsdp')
- wq_updated: float32 [2560, 2560], P('dp', 'fsdp')
- wq_copy: bfloat16 [2560, 2560], P('dp', 'fsdp')
- wkv_clipped: float32 [2560, 512], P('dp', 'fsdp')
- wkv_first_new: float32 [2560, 512], P('dp', 'fsdp')
- wkv_second_new: float32 [2560, 512], P('dp', 'fsdp')
- wkv_updated: float32 [2560, 512], P('dp', 'fsdp')
- wkv_copy: bfloat16 [2560, 512], P('dp', 'fsdp')
- wo_clipped: float32 [2560, 2560], P('dp', 'fsdp')
- wo_first_new: float32 [2560, 2560], P('dp', 'fsdp')
- wo_second_new: float32 [2560, 2560], P('dp', 'fsdp')
- wo_updated: float32 [2560, 2560], P('dp', 'fsdp')
- wo_copy: bfloat16 [2560, 2560], P('dp', 'fsdp')
- ffw_up_clipped: float32 [2, 2560, 7680], P(None, 'dp', 'fsdp')
- ffw_up_first_new: float32 [2, 2560, 7680], P(None, 'dp', 'fsdp')
- ffw_up_second_new: float32 [2, 2560, 7680], P(None, 'dp', 'fsdp')
- ffw_up_updated: float32 [2, 2560, 7680], P(None, 'dp', 'fsdp')
- ffw_up_copy: bfloat16 [2, 2560, 7680], P(None, 'dp', 'fsdp')
- ffw_down_clipped: float32 [7680, 2560], P('fsdp', 'dp')
- ffw_down_first_new: float32 [7680, 2560], P('fsdp', 'dp')
- ffw_down_second_new: float32 [7680, 2560], P('fsdp', 'dp')
- ffw_down_updated: float32 [7680, 2560], P('fsdp', 'dp')
- ffw_down_copy: bfloat16 [7680, 2560], P('fsdp', 'dp')
- vec_clipped: float32 [4, 2560], P(None, ('dp', 'fsdp'))
- vec_first_new: float32 [4, 2560], P(None, ('dp', 'fsdp'))
- vec_second_new: float32 [4, 2560], P(None, ('dp', 'fsdp'))
- vec_updated: float32 [4, 2560], P(None, ('dp', 'fsdp'))
- vec_copy: bfloat16 [4, 2560], P(None, ('dp', 'fsdp'))
Inputs may be any that keep to these rules, and one draw needn't show every extreme that they name: `seq_lengths`: row r lists the lengths of the sequences in buffer r in order, zeros after the last; slot 0 is never zero, every nonzero length is 64 or more, a row sums to at most 128, and some row holds one sequence of exactly 128 tokens.
All inputs are finite; a program needn't handle non-finite values.
Results may differ from a plain program's by a relative error of at most 0.02.
Values may be sent and summed in bfloat16 or wider, within the bound.
No kernel may reach another device: no remote copies, remote signals or barrier semaphores. Data moves between devices by JAX's collectives and lax.ppermute only.
A program may use at most 320 MiB of HBM per device.

v0:
```python
import jax
import jax.numpy as jnp
from jax import lax
from jax.sharding import PartitionSpec as P

D = 2560
H = 10
HD = 256
FF = 7680
WINDOW = 2048
STEP = 5


EPS_NORM = 1e-06
ROPE_BASE = 10000.0
NEG_BIG = -1e30
CLIP_NORM = 1.0
BETA_ONE = 0.5
BETA_TWO = 0.75
EPS_ADAM = 1e-08
DECAY_RATE = 0.1
LR_VECTOR = 0.3


def layout(lengths, tok_count):
    places = jnp.arange(tok_count, dtype=jnp.int32)
    end_at = jnp.cumsum(lengths)
    segment = jnp.sum((places[:, None] >= end_at[None, :]).astype(jnp.int32), axis=1)
    slot_ids = jnp.arange(lengths.shape[0], dtype=jnp.int32)
    start_of = jnp.sum(jnp.where(segment[:, None] > slot_ids[None, :], lengths[None, :], 0), axis=1)
    position = places - start_of
    valid_mask = (places < end_at[lengths.shape[0] - 1]).astype(jnp.float32)
    return (places, segment, position, valid_mask)


def rotate(values, position, orient):
    half_dim = values.shape[-1] // 2
    quarter = half_dim // 2
    exponent = jnp.arange(quarter, dtype=jnp.float32) * (2.0 / half_dim)
    angles = position.astype(jnp.float32)[:, None] / (ROPE_BASE**exponent)[None, :]
    cosine = jnp.cos(angles)[:, None, :]
    sine_vals = orient * jnp.sin(angles)[:, None, :]
    first_part = values[..., :quarter]
    second = values[..., quarter:half_dim]
    return jnp.concatenate(
        [
            first_part * cosine - second * sine_vals,
            second * cosine + first_part * sine_vals,
            values[..., half_dim:],
        ],
        axis=-1,
    )


def glu_mix(gate_lin, up_lin):
    return jax.nn.gelu(gate_lin, approximate=True) * up_lin


def attention_mask(places, segment):
    same_seg = segment[:, None] == segment[None, :]
    return (
        same_seg
        & (places[None, :] <= places[:, None])
        & (places[:, None] - places[None, :] < WINDOW)
    )


def adamw(gradient, first_mom, second_mom, weight, factor, step_rate):
    clipped = gradient * factor
    first_new = BETA_ONE * first_mom + (1.0 - BETA_ONE) * clipped
    second_new = BETA_TWO * second_mom + (1.0 - BETA_TWO) * clipped * clipped
    first_hat = first_new / (1.0 - BETA_ONE**STEP)
    second_hat = second_new / (1.0 - BETA_TWO**STEP)
    weight_new = weight - step_rate * (
        first_hat / (jnp.sqrt(second_hat) + EPS_ADAM) + DECAY_RATE * weight
    )
    return (clipped, first_new, second_new, weight_new, weight_new.astype(jnp.bfloat16))


def body(
    tokens,
    cotangent,
    seq_lengths,
    wq_master,
    wkv_master,
    wo_master,
    ffw_up_master,
    ffw_down_master,
    vec_master,
    wq_first,
    wq_second,
    wkv_first,
    wkv_second,
    wo_first,
    wo_second,
    ffw_up_first,
    ffw_up_second,
    ffw_down_first,
    ffw_down_second,
    vec_first,
    vec_second,
):
    wide_size = lax.axis_size("dp")
    narrow_size = lax.axis_size("fsdp")
    tok_count = tokens.shape[0]
    q_width = H * HD
    contract_rows = (((0,), (0,)), ((), ()))
    contract_cols = (((1,), (1,)), ((), ()))
    places, segment, position, valid_mask = layout(seq_lengths[0], tok_count)
    valid_col = valid_mask[:, None]
    shard_vec = vec_master.astype(jnp.bfloat16).reshape(4, 1, vec_master.shape[1])
    gathered = (
        lax.all_gather(wq_master.astype(jnp.bfloat16), "dp", axis=0, tiled=True),
        lax.all_gather(wkv_master.astype(jnp.bfloat16), "dp", axis=0, tiled=True),
        lax.all_gather(wo_master.astype(jnp.bfloat16), "dp", axis=0, tiled=True),
        lax.all_gather(ffw_up_master.astype(jnp.bfloat16), "dp", axis=1, tiled=True),
        lax.all_gather(ffw_down_master.astype(jnp.bfloat16), "dp", axis=1, tiled=True),
        lax.all_gather(shard_vec, "dp", axis=1, tiled=True),
    )
    wq_full, wkv_full, wo_full, vec_full = (
        lax.all_gather(gathered[0], "fsdp", axis=1, tiled=True),
        lax.all_gather(gathered[1], "fsdp", axis=1, tiled=True),
        lax.all_gather(gathered[2], "fsdp", axis=1, tiled=True),
        lax.all_gather(gathered[5], "fsdp", axis=2, tiled=True),
    )
    up_local = gathered[3]
    down_local = gathered[4]
    gate_weight = up_local[0]
    lin_weight = up_local[1]
    vec_full = vec_full.reshape(4, D).astype(jnp.float32)
    gain_one = vec_full[0]
    bias_one = vec_full[1]
    gain_two = vec_full[2]
    bias_two = vec_full[3]
    x_float = tokens.astype(jnp.float32)
    inverse = lax.rsqrt(jnp.mean(x_float * x_float, axis=1, keepdims=True) + EPS_NORM)
    normed = (x_float * inverse * gain_one[None, :]).astype(jnp.bfloat16)
    q_lin = jnp.dot(normed, wq_full, preferred_element_type=jnp.float32)
    kv_lin = jnp.dot(normed, wkv_full, preferred_element_type=jnp.float32)
    queries = (rotate(q_lin.reshape(tok_count, H, HD), position, 1.0) * HD ** (-0.5)).astype(
        jnp.bfloat16
    )
    keys_rot = rotate(kv_lin[:, None, :HD], position, 1.0)[:, 0, :].astype(jnp.bfloat16)
    values_low = kv_lin[:, HD:].astype(jnp.bfloat16)
    allowed = attention_mask(places, segment)
    scores = jnp.einsum("qhe,ke->hqk", queries, keys_rot, preferred_element_type=jnp.float32)
    scores = jnp.where(allowed[None], scores, NEG_BIG)
    row_peak = jnp.max(scores, axis=-1, keepdims=True)
    raised = jnp.exp(scores - row_peak)
    total_sum = jnp.sum(raised, axis=-1, keepdims=True)
    prob_low = (raised / total_sum).astype(jnp.bfloat16)
    log_totals = row_peak + jnp.log(total_sum)
    attended_parts = jnp.einsum(
        "hqk,ke->qhe", prob_low, values_low, preferred_element_type=jnp.float32
    ).astype(jnp.bfloat16)
    attended = attended_parts.reshape(tok_count, q_width)
    mixed = x_float + valid_col * (
        jnp.dot(attended, wo_full, preferred_element_type=jnp.float32) + bias_one[None, :]
    )
    inv_two = lax.rsqrt(jnp.mean(mixed * mixed, axis=1, keepdims=True) + EPS_NORM)
    normed_two = (mixed * inv_two * gain_two[None, :]).astype(jnp.bfloat16)
    grad_out = cotangent.astype(jnp.float32) * valid_col
    grad_low = grad_out.astype(jnp.bfloat16)
    group_normed, group_grad = (
        lax.all_gather(normed_two, "fsdp", axis=0, tiled=True),
        lax.all_gather(grad_low, "fsdp", axis=0, tiled=True),
    )
    gate_lin = jnp.dot(group_normed, gate_weight, preferred_element_type=jnp.float32)
    up_lin = jnp.dot(group_normed, lin_weight, preferred_element_type=jnp.float32)
    hidden = glu_mix(gate_lin, up_lin).astype(jnp.bfloat16)
    ffw_term = lax.psum_scatter(
        jnp.dot(hidden, down_local, preferred_element_type=jnp.float32).astype(jnp.bfloat16),
        "fsdp",
        scatter_dimension=0,
        tiled=True,
    ).astype(jnp.float32)
    block_out = (mixed + valid_col * (ffw_term + bias_two[None, :])).astype(jnp.bfloat16)
    bias_two_grad = jnp.sum(grad_out, axis=0)
    down_grad = lax.dot_general(
        hidden, group_grad, contract_rows, preferred_element_type=jnp.float32
    )
    hidden_grad = lax.dot_general(
        group_grad, down_local, contract_cols, preferred_element_type=jnp.float32
    )
    unused_value, pullback = jax.vjp(glu_mix, gate_lin, up_lin)
    gate_grad, lin_grad = pullback(hidden_grad)
    gate_low = gate_grad.astype(jnp.bfloat16)
    lin_low = lin_grad.astype(jnp.bfloat16)
    up_grad = jnp.stack(
        [
            lax.dot_general(
                group_normed, gate_low, contract_rows, preferred_element_type=jnp.float32
            ),
            lax.dot_general(
                group_normed, lin_low, contract_rows, preferred_element_type=jnp.float32
            ),
        ]
    )
    first_term = lax.dot_general(
        gate_low, gate_weight, contract_cols, preferred_element_type=jnp.float32
    )
    normed_two_grad = lax.psum_scatter(
        first_term
        + lax.dot_general(lin_low, lin_weight, contract_cols, preferred_element_type=jnp.float32),
        "fsdp",
        scatter_dimension=0,
        tiled=True,
    )
    gain_two_grad = jnp.sum(normed_two_grad * mixed * inv_two, axis=0)
    scaled_two = normed_two_grad * gain_two[None, :]
    mixed_grad = (
        inv_two
        * (
            scaled_two
            - mixed * inv_two * inv_two * jnp.mean(scaled_two * mixed, axis=1, keepdims=True)
        )
        + grad_out
    )
    branch_low = (mixed_grad * valid_col).astype(jnp.bfloat16)
    bias_one_grad = jnp.sum(branch_low.astype(jnp.float32), axis=0)
    wo_grad = lax.dot_general(
        attended, branch_low, contract_rows, preferred_element_type=jnp.float32
    )
    attn_grad = (
        lax.dot_general(branch_low, wo_full, contract_cols, preferred_element_type=jnp.float32)
        .astype(jnp.bfloat16)
        .reshape(tok_count, H, HD)
    )
    allowed = attention_mask(places, segment)
    scores = jnp.einsum("qhe,ke->hqk", queries, keys_rot, preferred_element_type=jnp.float32)
    scores = jnp.where(allowed[None], scores, NEG_BIG)
    probs = jnp.exp(scores - log_totals)
    prob_low = probs.astype(jnp.bfloat16)
    grad_prob = jnp.einsum("qhe,ke->hqk", attn_grad, values_low, preferred_element_type=jnp.float32)
    value_part = jnp.einsum("hqk,qhe->ke", prob_low, attn_grad, preferred_element_type=jnp.float32)
    row_delta = jnp.sum(probs * grad_prob, axis=-1, keepdims=True)
    grad_score = (probs * (grad_prob - row_delta)).astype(jnp.bfloat16)
    query_parts = jnp.einsum(
        "hqk,ke->qhe", grad_score, keys_rot, preferred_element_type=jnp.float32
    )
    key_part = jnp.einsum("hqk,qhe->ke", grad_score, queries, preferred_element_type=jnp.float32)
    q_grad = (
        (rotate(query_parts, position, -1.0) * HD ** (-0.5))
        .astype(jnp.bfloat16)
        .reshape(tok_count, q_width)
    )
    key_grad = rotate(key_part[:, None, :], position, -1.0)[:, 0, :]
    kv_grad = jnp.concatenate([key_grad, value_part], axis=1).astype(jnp.bfloat16)
    wq_grad = lax.dot_general(normed, q_grad, contract_rows, preferred_element_type=jnp.float32)
    wkv_grad = lax.dot_general(normed, kv_grad, contract_rows, preferred_element_type=jnp.float32)
    normed_grad = lax.dot_general(
        q_grad, wq_full, contract_cols, preferred_element_type=jnp.float32
    )
    normed_grad = normed_grad + lax.dot_general(
        kv_grad, wkv_full, contract_cols, preferred_element_type=jnp.float32
    )
    gain_one_grad = jnp.sum(normed_grad * x_float * inverse, axis=0)
    scaled = normed_grad * gain_one[None, :]
    input_grad = (
        inverse
        * (scaled - x_float * inverse * inverse * jnp.mean(scaled * x_float, axis=1, keepdims=True))
        + mixed_grad
    ).astype(jnp.bfloat16)
    vec_grad = jnp.stack([gain_one_grad, bias_one_grad, gain_two_grad, bias_two_grad]).reshape(
        4, wide_size, narrow_size, D // (wide_size * narrow_size)
    )
    summed = (
        lax.psum_scatter(
            up_grad.astype(jnp.bfloat16), "dp", scatter_dimension=1, tiled=True
        ).astype(jnp.float32),
        lax.psum_scatter(
            down_grad.astype(jnp.bfloat16), "dp", scatter_dimension=1, tiled=True
        ).astype(jnp.float32),
        lax.psum_scatter(
            wq_grad.astype(jnp.bfloat16), "dp", scatter_dimension=0, tiled=True
        ).astype(jnp.float32),
        lax.psum_scatter(
            wkv_grad.astype(jnp.bfloat16), "dp", scatter_dimension=0, tiled=True
        ).astype(jnp.float32),
        lax.psum_scatter(
            wo_grad.astype(jnp.bfloat16), "dp", scatter_dimension=0, tiled=True
        ).astype(jnp.float32),
        lax.psum_scatter(
            vec_grad.astype(jnp.bfloat16), "dp", scatter_dimension=1, tiled=True
        ).astype(jnp.float32),
    )
    attn_sums = (
        lax.psum_scatter(summed[2], "fsdp", scatter_dimension=1, tiled=True),
        lax.psum_scatter(summed[3], "fsdp", scatter_dimension=1, tiled=True),
        lax.psum_scatter(summed[4], "fsdp", scatter_dimension=1, tiled=True),
        lax.psum_scatter(summed[5], "fsdp", scatter_dimension=2, tiled=True),
    )
    own_up = summed[0]
    own_down = summed[1]
    own_q = attn_sums[0]
    own_kv = attn_sums[1]
    own_o = attn_sums[2]
    own_vec = attn_sums[3].reshape(4, attn_sums[3].shape[3])
    local_squares = jnp.sum(own_q * own_q) + jnp.sum(own_kv * own_kv) + jnp.sum(own_o * own_o)
    local_squares = (
        local_squares
        + jnp.sum(own_up * own_up)
        + jnp.sum(own_down * own_down)
        + jnp.sum(own_vec * own_vec)
    )
    total_squares = lax.psum(local_squares, ("dp", "fsdp"))
    grad_norm = jnp.sqrt(total_squares)
    factor = jnp.minimum(1.0, CLIP_NORM / grad_norm)
    q_out = adamw(own_q, wq_first, wq_second, wq_master, factor, D ** (-0.5))
    kv_out = adamw(own_kv, wkv_first, wkv_second, wkv_master, factor, D ** (-0.5))
    o_out = adamw(own_o, wo_first, wo_second, wo_master, factor, (H * HD // 32) ** (-0.5))
    up_out = adamw(own_up, ffw_up_first, ffw_up_second, ffw_up_master, factor, D ** (-0.5))
    down_out = adamw(
        own_down, ffw_down_first, ffw_down_second, ffw_down_master, factor, FF ** (-0.5)
    )
    vec_out = adamw(own_vec, vec_first, vec_second, vec_master, factor, LR_VECTOR)
    return (
        block_out,
        input_grad,
        grad_norm,
        q_out[0],
        q_out[1],
        q_out[2],
        q_out[3],
        q_out[4],
        kv_out[0],
        kv_out[1],
        kv_out[2],
        kv_out[3],
        kv_out[4],
        o_out[0],
        o_out[1],
        o_out[2],
        o_out[3],
        o_out[4],
        up_out[0],
        up_out[1],
        up_out[2],
        up_out[3],
        up_out[4],
        down_out[0],
        down_out[1],
        down_out[2],
        down_out[3],
        down_out[4],
        vec_out[0],
        vec_out[1],
        vec_out[2],
        vec_out[3],
        vec_out[4],
    )


def solution(mesh):
    placed = (
        P(("dp", "fsdp"), None),
        P(("dp", "fsdp"), None),
        P(("dp", "fsdp"), None),
        P("dp", "fsdp"),
        P("dp", "fsdp"),
        P("dp", "fsdp"),
        P(None, "dp", "fsdp"),
        P("fsdp", "dp"),
        P(None, ("dp", "fsdp")),
        P("dp", "fsdp"),
        P("dp", "fsdp"),
        P("dp", "fsdp"),
        P("dp", "fsdp"),
        P("dp", "fsdp"),
        P("dp", "fsdp"),
        P(None, "dp", "fsdp"),
        P(None, "dp", "fsdp"),
        P("fsdp", "dp"),
        P("fsdp", "dp"),
        P(None, ("dp", "fsdp")),
        P(None, ("dp", "fsdp")),
    )
    return jax.shard_map(
        body,
        mesh=mesh,
        in_specs=placed,
        out_specs=(
            P(("dp", "fsdp"), None),
            P(("dp", "fsdp"), None),
            P(),
            P("dp", "fsdp"),
            P("dp", "fsdp"),
            P("dp", "fsdp"),
            P("dp", "fsdp"),
            P("dp", "fsdp"),
            P("dp", "fsdp"),
            P("dp", "fsdp"),
            P("dp", "fsdp"),
            P("dp", "fsdp"),
            P("dp", "fsdp"),
            P("dp", "fsdp"),
            P("dp", "fsdp"),
            P("dp", "fsdp"),
            P("dp", "fsdp"),
            P("dp", "fsdp"),
            P(None, "dp", "fsdp"),
            P(None, "dp", "fsdp"),
            P(None, "dp", "fsdp"),
            P(None, "dp", "fsdp"),
            P(None, "dp", "fsdp"),
            P("fsdp", "dp"),
            P("fsdp", "dp"),
            P("fsdp", "dp"),
            P("fsdp", "dp"),
            P("fsdp", "dp"),
            P(None, ("dp", "fsdp")),
            P(None, ("dp", "fsdp")),
            P(None, ("dp", "fsdp")),
            P(None, ("dp", "fsdp")),
            P(None, ("dp", "fsdp")),
        ),
        check_vma=False,
    )
```

profile of v0, /device:TPU:0, one launch (start us, length us, event | category | flops | bytes accessed | tf_op | source)
XLA Modules:
  0.0 1779.6 jit_solution(18189431976985066989)
XLA Ops:
  11.4 12.6 all_gather.38
  24.1 22.0 %all-gather.14.cloned.1.call-done = bf16[2560,640]{1,0:T(8,128)(2,1)} async-done(((bf16[320,640]{1,0:T(8,128)(2,1)}), bf16[2560,640]{1,0:T(8,128)(2,1)}) %all-gather.14.cloned.1.call-update) | async-done | bytes 3276816 | tf_op jit(solution)/shard_map/all_gather | solution.py:113
  46.2 35.3 %all-gather.18.cloned.1.call-done = bf16[2560,640]{1,0:T(8,128)(2,1)} async-done(((bf16[320,640]{1,0:T(8,128)(2,1)}), bf16[2560,640]{1,0:T(8,128)(2,1)}) %all-gather.18.cloned.1.call-update) | async-done | bytes 3276816 | tf_op jit(solution)/shard_map/all_gather | solution.py:115
  82.3 8.8 all-gather.1
  91.5 23.7 %all_gather.37 = bf16[4,8,320]{1,0,2:T(4,128)(2,1)S(1)} all-gather(bf16[4,8,80]{1,0,2:T(4,128)(2,1)S(1)} %copy.119), channel_id=1, replica_groups=mesh['dp'=8,'fsdp'=4] {'fsdp'}, dimensions={2}, use_global_device_ids=true | all-gather | bytes 25600 | tf_op jit(solution)/shard_map/all_gather | solution.py:124
  121.3 21.9 %all-gather.12.cloned.1.call-done = bf16[2560,512]{1,0:T(8,128)(2,1)} async-done(((bf16[2560,128]{1,0:T(8,128)(2,1)}), bf16[2560,512]{1,0:T(8,128)(2,1)}) %all-gather.12.cloned.1.call-update) | async-done | bytes 2621456 | tf_op jit(solution)/shard_map/all_gather | solution.py:122
  147.1 222.5 %all-gather.16.cloned.1.call-done = bf16[2560,2560]{1,0:T(8,128)(2,1)} async-done(((bf16[2560,640]{1,0:T(8,128)(2,1)}), bf16[2560,2560]{1,0:T(8,128)(2,1)}) %all-gather.16.cloned.1.call-update) | async-done | bytes 13107216 | tf_op jit(solution)/shard_map/all_gather | solution.py:121
  369.6 8.3 fusion.63
  384.4 211.6 %all-gather.20.cloned.1.call-done = bf16[2560,2560]{1,0:T(8,128)(2,1)} async-done(((bf16[2560,640]{1,0:T(8,128)(2,1)}), bf16[2560,2560]{1,0:T(8,128)(2,1)}) %all-gather.20.cloned.1.call-update) | async-done | bytes 13107216 | tf_op jit(solution)/shard_map/all_gather | solution.py:123
  596.0 6.8 multiply_reduce_fusion.2
  604.0 4.1 convert_element_type.184
  614.7 42.4 %all-gather.22.cloned.1.call-done = bf16[512,2560]{1,0:T(8,128)(2,1)} async-done(((bf16[128,2560]{1,0:T(8,128)(2,1)}), bf16[512,2560]{1,0:T(8,128)(2,1)}) %all-gather.22.cloned.1.call-update) | async-done | bytes 2621456 | tf_op jit(solution)/shard_map/all_gather | solution.py:165
  657.1 103.3 %all-gather.24.cloned.1.call-done = bf16[2,2560,1920]{2,1,0:T(8,128)(2,1)} async-done(((bf16[2,320,1920]{2,1,0:T(8,128)(2,1)}), bf16[2,2560,1920]{2,1,0:T(8,128)(2,1)}) %all-gather.24.cloned.1.call-update) | async-done | bytes 19660816 | tf_op jit(solution)/shard_map/all_gather | solution.py:116
  760.4 11.4 fusion.5
  773.1 7.5 fusion.3
  780.6 36.8 %all-gather.28.cloned.1.call-done = bf16[512,2560]{1,0:T(8,128)(2,1)} async-done(((bf16[128,2560]{1,0:T(8,128)(2,1)}), bf16[512,2560]{1,0:T(8,128)(2,1)}) %all-gather.28.cloned.1.call-update) | async-done | bytes 2621456 | tf_op jit(solution)/shard_map/all_gather | solution.py:166
  817.4 61.8 %all-gather.26.cloned.1.call-done = bf16[1920,2560]{0,1:T(8,128)(2,1)} async-done(((bf16[1920,320]{0,1:T(8,128)(2,1)}), bf16[1920,2560]{0,1:T(8,128)(2,1)}) %all-gather.26.cloned.1.call-update) | async-done | bytes 9830416 | tf_op jit(solution)/shard_map/all_gather | solution.py:117
  879.2 15.3 multiply_convert_fusion
  895.7 6.9 convolution_convert_fusion.6
  903.1 9.0 fusion.2
  912.1 9.8 fusion.6
  923.7 31.2 %reduce-scatter.12.cloned.1.call-done = bf16[128,2560]{1,0:T(8,128)(2,1)} async-done(((bf16[512,2560]{1,0:T(8,128)(2,1)}), bf16[128,2560]{1,0:T(8,128)(2,1)}) %reduce-scatter.12.cloned.1.call-update) | async-done | bytes 655376 | tf_op jit(solution)/shard_map/reduce_scatter | solution.py:171
  954.9 95.8 %reduce-scatter.14.cloned.1.call-done = f32[128,2560]{1,0:T(8,128)} async-done(((f32[512,2560]{1,0:T(8,128)}), f32[128,2560]{1,0:T(8,128)}) %reduce-scatter.14.cloned.1.call-update) | async-done | bytes 1310736 | tf_op jit(solution)/shard_map/reduce_scatter | solution.py:202
  1050.7 3.6 multiply_reduce_fusion
  1057.7 9.0 convolution_convert_fusion.7
  1075.2 7.0 convolution_convert_fusion.1
  1083.4 6.6 convolution_convert_fusion
  1091.6 10.3 convolution_convert_fusion.2
  1103.5 10.4 fusion.1
  1113.8 3.7 reduce-scatter.20.cloned.1.call-done
  1119.7 7.8 fusion
  1127.6 13.5 pad_maximum_fusion
  1141.1 75.2 %reduce-scatter.16.cloned.1.call-done = bf16[320,2560]{1,0:T(8,128)(2,1)} async-done(((bf16[2560,2560]{1,0:T(8,128)(2,1)}), bf16[320,2560]{1,0:T(8,128)(2,1)}) %reduce-scatter.16.cloned.1.call-update) | async-done | bytes 1638416 | tf_op jit(solution)/shard_map/reduce_scatter | solution.py:274
  1216.3 3.5 convert_element_type.202
  1220.0 95.1 %reduce-scatter.24.cloned.1.call-done = bf16[320,2560]{1,0:T(8,128)(2,1)} async-done(((bf16[2560,2560]{1,0:T(8,128)(2,1)}), bf16[320,2560]{1,0:T(8,128)(2,1)}) %reduce-scatter.24.cloned.1.call-update) | async-done | bytes 1638416 | tf_op jit(solution)/shard_map/reduce_scatter | solution.py:280
  1320.7 10.1 fusion.83
  1332.1 22.8 %all-reduce = bf16[4,8,4,80]{3,2,1,0:T(4,128)(2,1)S(1)} all-reduce(bf16[4,8,4,80]{3,2,1,0:T(4,128)(2,1)S(1)} %pad_maximum_fusion.4), channel_id=13, replica_groups=mesh['dp'=8,'fsdp'=4] {'dp'}, use_global_device_ids=true, to_apply=%region_29.30.clone | all-reduce | flops 10240 | bytes 40960
  1355.6 11.8 all-reduce.1
  1368.7 28.2 %reduce-scatter.30.cloned.1.call-done = bf16[1920,320]{0,1:T(8,128)(2,1)} async-done(((bf16[1920,2560]{0,1:T(8,128)(2,1)}), bf16[1920,320]{0,1:T(8,128)(2,1)}) %reduce-scatter.30.cloned.1.call-update) | async-done | bytes 1228816 | tf_op jit(solution)/shard_map/reduce_scatter | solution.py:271
  1399.4 22.3 %reduce-scatter.22.cloned.1.call-done = f32[320,128]{1,0:T(8,128)} async-done(((f32[320,512]{1,0:T(8,128)}), f32[320,128]{1,0:T(8,128)}) %reduce-scatter.22.cloned.1.call-update) | async-done | bytes 163856 | tf_op jit(solution)/shard_map/reduce_scatter | solution.py:289
  1423.3 130.5 %reduce-scatter.28.cloned.1.call-done = bf16[2,320,1920]{2,1,0:T(8,128)(2,1)} async-done(((bf16[2,2560,1920]{2,1,0:T(8,128)(2,1)}), bf16[2,320,1920]{2,1,0:T(8,128)(2,1)}) %reduce-scatter.28.cloned.1.call-update) | async-done | bytes 2457616 | tf_op jit(solution)/shard_map/reduce_scatter | solution.py:268
  1553.9 3.6 fusion.7
  1557.4 61.5 %reduce-scatter.18.cloned.1.call-done = f32[320,640]{1,0:T(8,128)} async-done(((f32[320,2560]{1,0:T(8,128)}), f32[320,640]{1,0:T(8,128)}) %reduce-scatter.18.cloned.1.call-update) | async-done | bytes 819216 | tf_op jit(solution)/shard_map/reduce_scatter | solution.py:288
  1622.2 62.0 %reduce-scatter.26.cloned.1.call-done = f32[320,640]{1,0:T(8,128)} async-done(((f32[320,2560]{1,0:T(8,128)}), f32[320,640]{1,0:T(8,128)}) %reduce-scatter.26.cloned.1.call-update) | async-done | bytes 819216 | tf_op jit(solution)/shard_map/reduce_scatter | solution.py:290
  1690.1 40.5 %psum.7 = f32[]{:T(128)} all-reduce(f32[]{:T(128)S(6)} %add.239), channel_id=1, replica_groups=mesh['dp'=8,'fsdp'=4] {'dp','fsdp'}, use_global_device_ids=true, to_apply=%region_32.33 | all-reduce | flops 1 | bytes 8 | tf_op jit(solution)/shard_map/psum | solution.py:306
  1736.8 5.7 fusion.73
  1746.2 7.3 fusion.69
  1757.0 10.8 fusion.71
  (278 shorter events, 86.6 us)
Async XLA Ops:
  7.2 38.9 %all-gather.14.cloned.1.call-start = ((), (), s32[]{:S(2)}) async-start(), calls=%async_computation.11 | async-start | bytes 3686400 | tf_op jit(solution)/shard_map/all_gather | solution.py:113
  9.3 72.2 %all-gather.18.cloned.1.call-start = ((), (), s32[]{:S(2)}) async-start(), calls=%async_computation.13 | async-start | bytes 3686400 | tf_op jit(solution)/shard_map/all_gather | solution.py:115
  11.3 131.9 %all-gather.12.cloned.1.call-start = ((), (), s32[]{:S(2)}) async-start(), calls=%async_computation.10 | async-start | bytes 3276800 | tf_op jit(solution)/shard_map/all_gather | solution.py:122
  24.0 345.5 %all-gather.16.cloned.1.call-start = ((), (), s32[]{:S(2)}) async-start(), calls=%async_computation.12 | async-start | bytes 16384000 | tf_op jit(solution)/shard_map/all_gather | solution.py:121
  46.1 35.4 %copy-start.63 = (s32[1,2]{1,0:T(1,128)S(1)}, s32[1,2]{1,0:T(1,128)}, u32[]{:S(2)}) copy-start(s32[1,2]{1,0:T(1,128)} %param.23) | copy-start | bytes 28
  46.2 36.2 %copy-start.51 = (f32[4,80]{1,0:T(4,128)S(1)}, f32[4,80]{1,0:T(4,128)}, u32[]{:S(2)}) copy-start(f32[4,80]{1,0:T(4,128)} %param.29) | copy-start | bytes 3844
  46.2 549.8 %all-gather.20.cloned.1.call-start = ((), (), s32[]{:S(2)}) async-start(), calls=%async_computation.14 | async-start | bytes 16384000 | tf_op jit(solution)/shard_map/all_gather | solution.py:123
  81.5 37.9 %copy-start = (bf16[128,2560]{1,0:T(8,128)(2,1)S(1)}, bf16[128,2560]{1,0:T(8,128)(2,1)}, u32[]{:S(2)}) copy-start(bf16[128,2560]{1,0:T(8,128)(2,1)} %param.21) | copy-start | bytes 1966084
  81.5 575.6 %all-gather.22.cloned.1.call-start = ((), (), s32[]{:S(2)}) async-start(), calls=%async_computation.15 | async-start | bytes 3276800 | tf_op jit(solution)/shard_map/all_gather | solution.py:165
  118.0 28.2 %copy-start.53 = (f32[64]{0:T(128)}, f32[64]{0:T(128)S(1)}, u32[]{:S(2)}) copy-start(f32[64]{0:T(128)S(1)} %multiply_power_fusion) | copy-start | bytes 772
  119.6 258.3 %copy-start.55 = (f32[128]{0:T(128)}, f32[128]{0:T(128)S(1)}, u32[]{:S(2)}) copy-start(f32[128]{0:T(128)S(1)} %subtract_convert_fusion.2) | copy-start | bytes 1540
  383.7 212.3 %copy-start.40 = (f32[10,128]{1,0:T(8,128)}, f32[10,128]{1,0:T(8,128)S(1)}, u32[]{:S(2)}) copy-start(f32[10,128]{1,0:T(8,128)S(1)} %get-tuple-element.87) | copy-start | bytes 15364
  384.0 212.0 %copy-start.43 = (f32[10,128]{1,0:T(8,128)}, f32[10,128]{1,0:T(8,128)S(1)}, u32[]{:S(2)}) copy-start(f32[10,128]{1,0:T(8,128)S(1)} %fusion.40) | copy-start | bytes 15364
  384.4 218.4 %copy-start.16 = (bf16[256,10,128]{2,0,1:T(8,128)(2,1)}, bf16[256,10,128]{2,0,1:T(8,128)(2,1)S(1)}, u32[]{:S(2)}) copy-start(bf16[256,10,128]{2,0,1:T(8,128)(2,1)S(1)} %convolution_convert_fusion.8) | copy-start | bytes 1966084
  603.9 156.5 %all-gather.24.cloned.1.call-start = ((), (), s32[]{:S(2)}) async-start(), calls=%async_computation.16 | async-start | bytes 22118400 | tf_op jit(solution)/shard_map/all_gather | solution.py:116
  608.1 209.3 %all-gather.28.cloned.1.call-start = ((), (), s32[]{:S(2)}) async-start(), calls=%async_computation.19 | async-start | bytes 3276800 | tf_op jit(solution)/shard_map/all_gather | solution.py:166
  611.5 267.6 %all-gather.26.cloned.1.call-start = ((), (), s32[]{:S(2)}) async-start(), calls=%async_computation.17 | async-start | bytes 11059200 | tf_op jit(solution)/shard_map/all_gather | solution.py:117
  614.5 340.4 %reduce-scatter.12.cloned.1.call-start = ((), (), s32[]{:S(2)}) async-start(), calls=%async_computation.18 | async-start | bytes 3276800 | tf_op jit(solution)/shard_map/reduce_scatter | solution.py:171
  760.4 11.5 copy-start.60
  760.4 12.7 copy-start.62
  879.2 16.6 copy-start.61
  902.6 148.0 %reduce-scatter.14.cloned.1.call-start = ((), (), s32[]{:S(2)}) async-start(), calls=%async_computation.20 | async-start | bytes 6553600 | tf_op jit(solution)/shard_map/reduce_scatter | solution.py:202
  903.1 9.0 copy-start.66
  922.0 128.7 %copy-start.34 = (f32[2560]{0:T(1024)S(1)}, f32[2560]{0:T(1024)}, u32[]{:S(2)}) copy-start(f32[2560]{0:T(1024)} %mul.575) | copy-start | bytes 30724
  922.0 128.7 %copy-start.48 = (f32[128]{0:T(128)S(1)}, f32[128]{0:T(128)}, u32[]{:S(2)}) copy-start(f32[128]{0:T(128)} %compare_convert_fusion.1) | copy-start | bytes 1540
  922.0 128.7 %copy-start.58 = (f32[128]{0:T(128)S(1)}, f32[128]{0:T(128)}, u32[]{:S(2)}) copy-start(f32[128]{0:T(128)} %copy-done.57) | copy-start | bytes 1540
  922.0 195.6 %reduce-scatter.20.cloned.1.call-start = ((), (), s32[]{:S(2)}) async-start(), calls=%async_computation.23 | async-start | bytes 2949120 | tf_op jit(solution)/shard_map/reduce_scatter | solution.py:277
  1073.2 143.1 %reduce-scatter.16.cloned.1.call-start = ((), (), s32[]{:S(2)}) async-start(), calls=%async_computation.21 | async-start | bytes 14745600 | tf_op jit(solution)/shard_map/reduce_scatter | solution.py:274
  1082.3 232.7 %reduce-scatter.24.cloned.1.call-start = ((), (), s32[]{:S(2)}) async-start(), calls=%async_computation.25 | async-start | bytes 14745600 | tf_op jit(solution)/shard_map/reduce_scatter | solution.py:280
  1090.0 306.9 %reduce-scatter.30.cloned.1.call-start = ((), (), s32[]{:S(2)}) async-start(), calls=%async_computation.28 | async-start | bytes 11059200 | tf_op jit(solution)/shard_map/reduce_scatter | solution.py:271
  1101.9 319.8 %reduce-scatter.22.cloned.1.call-start = ((), (), s32[]{:S(2)}) async-start(), calls=%async_computation.24 | async-start | bytes 819200 | tf_op jit(solution)/shard_map/reduce_scatter | solution.py:289
  1119.5 434.4 %reduce-scatter.28.cloned.1.call-start = ((), (), s32[]{:S(2)}) async-start(), calls=%async_computation.27 | async-start | bytes 22118400 | tf_op jit(solution)/shard_map/reduce_scatter | solution.py:268
  1141.1 477.8 %reduce-scatter.18.cloned.1.call-start = ((), (), s32[]{:S(2)}) async-start(), calls=%async_computation.22 | async-start | bytes 4096000 | tf_op jit(solution)/shard_map/reduce_scatter | solution.py:288
  1219.9 464.3 %reduce-scatter.26.cloned.1.call-start = ((), (), s32[]{:S(2)}) async-start(), calls=%async_computation.26 | async-start | bytes 4096000 | tf_op jit(solution)/shard_map/reduce_scatter | solution.py:290
  1320.7 10.1 copy-start.2
  1320.7 10.1 copy-start.28
  1368.7 320.1 %copy-start.13 = (f32[128,2560]{1,0:T(8,128)S(1)}, f32[128,2560]{1,0:T(8,128)}, u32[]{:S(2)}) copy-start(f32[128,2560]{1,0:T(8,128)} %get-tuple-element.63) | copy-start | bytes 3932164
  1620.9 110.5 %copy-start.49 = (f32[4,80]{1,0:T(4,128)S(1)}, f32[4,80]{1,0:T(4,128)}, u32[]{:S(2)}) copy-start(f32[4,80]{1,0:T(4,128)} %param.40) | copy-start | bytes 3844
  1620.9 110.5 %copy-start.52 = (f32[4,80]{1,0:T(4,128)S(1)}, f32[4,80]{1,0:T(4,128)}, u32[]{:S(2)}) copy-start(f32[4,80]{1,0:T(4,128)} %param.29) | copy-start | bytes 3844
  1620.9 110.5 %copy-start.59 = (f32[4,80]{1,0:T(4,128)S(1)}, f32[4,80]{1,0:T(4,128)}, u32[]{:S(2)}) copy-start(f32[4,80]{1,0:T(4,128)} %param.41) | copy-start | bytes 3844
  1620.9 112.3 %copy-start.24 = (f32[320,128]{1,0:T(8,128)S(1)}, f32[320,128]{1,0:T(8,128)}, u32[]{:S(2)}) copy-start(f32[320,128]{1,0:T(8,128)} %reduce-scatter.22.cloned.1.call-done) | copy-start | bytes 491524
  1732.6 9.9 copy-start.50
  1735.2 7.4 copy-start.26
  1736.8 7.8 copy-start.15
  1742.6 13.4 slice-start
  1742.6 13.4 slice-start.2
  1746.2 9.9 slice-start.1
  1746.2 9.9 slice-start.3
  (45 other events, 111.9 us)
Sparse Core Ops, SparseCore 0:
  10.5 35.5 all-gather.13
  48.6 32.8 all-gather.17
  83.0 60.1 all-gather.11
  144.6 224.9 all-gather.15
  371.0 224.9 all-gather.19
  604.0 52.9 all-gather.21
  659.5 100.8 all-gather.23
  762.5 54.7 all-gather.27
  819.9 59.2 all-gather.25
  902.7 52.0 reduce-scatter.11
  957.2 93.4 reduce-scatter.13
  1073.4 44.1 reduce-scatter.19
  1121.1 95.1 reduce-scatter.15
  1219.8 95.1 reduce-scatter.23
  1318.4 78.4 reduce-scatter.29
  1399.6 22.0 reduce-scatter.21
  1425.3 128.5 reduce-scatter.27
  1556.6 62.2 reduce-scatter.17
  1621.8 62.3 reduce-scatter.25
where the time goes:
time: 1790 us; the launch traced here: 1780 us
  waiting for transfers between devices  1360 us (76%)
  matrix products  147 us (8%)
  blocking collectives  120 us (7%)
  other arithmetic  102 us (6%)
  local copies, waits for them, and re-layouts  24.6 us (1%)
  between operations  21.2 us (1%)
    all_gather x1, waiting for transfers between devices, body(): lax.all_gather(gathered[0], 'fsdp', axis=1, tiled=True)  223 us
    all_gather x1, waiting for transfers between devices, body(): lax.all_gather(gathered[2], 'fsdp', axis=1, tiled=True)  212 us
    reduce_scatter x1, waiting for transfers between devices, body(): lax.psum_scatter(up_grad.astype(jnp.bfloat16), 'dp', scatter_dimension=1,...  131 us
    all_gather x1, waiting for transfers between devices, body(): lax.all_gather(ffw_up_master.astype(jnp.bfloat16), 'dp', axis=1, tiled=True)  103 us
    reduce_scatter x1, waiting for transfers between devices, body(): lax.psum_scatter(first_term + lax.dot_general(lin_low, lin_weight, contra...  95.8 us
    reduce_scatter x1, waiting for transfers between devices, body(): lax.psum_scatter(wo_grad.astype(jnp.bfloat16), 'dp', scatter_dimension=0,...  95.1 us
    reduce_scatter x1, waiting for transfers between devices, body(): lax.psum_scatter(wq_grad.astype(jnp.bfloat16), 'dp', scatter_dimension=0,...  75.2 us
    reduce_scatter x1, waiting for transfers between devices, body(): lax.psum_scatter(summed[4], 'fsdp', scatter_dimension=1, tiled=True)  62 us
  transfers between devices with their start and end apart: 19, of which 19 were waited for; matrix products, arithmetic and copies ran while one was open for 9% of the time, Pallas kernels for 0%

commit v1 on v0

v1 whole, which is shorter than its diff:
```python
import functools
import math

import jax
import jax.numpy as jnp
from jax import lax
from jax.experimental import pallas as pl
from jax.experimental.pallas import tpu as pltpu
from jax.sharding import PartitionSpec as P

D = 2560
H = 10
HD = 256
FF = 7680
WINDOW = 2048
STEP = 5


EPS_NORM = 1e-06
ROPE_BASE = 10000.0
NEG_BIG = -1e30
CLIP_NORM = 1.0
BETA_ONE = 0.5
BETA_TWO = 0.75
EPS_ADAM = 1e-08
DECAY_RATE = 0.1
LR_VECTOR = 0.3


def layout(lengths, tok_count):
    places = jnp.arange(tok_count, dtype=jnp.int32)
    end_at = jnp.cumsum(lengths)
    segment = jnp.sum((places[:, None] >= end_at[None, :]).astype(jnp.int32), axis=1)
    slot_ids = jnp.arange(lengths.shape[0], dtype=jnp.int32)
    start_of = jnp.sum(jnp.where(segment[:, None] > slot_ids[None, :], lengths[None, :], 0), axis=1)
    position = places - start_of
    valid_mask = (places < end_at[lengths.shape[0] - 1]).astype(jnp.float32)
    return (places, segment, position, valid_mask)


def angle_tables(position):
    half_dim = HD // 2
    quarter = half_dim // 2
    exponent = jnp.arange(quarter, dtype=jnp.float32) * (2.0 / half_dim)
    angles = position.astype(jnp.float32)[:, None] / (ROPE_BASE**exponent)[None, :]
    cosine = jnp.cos(angles)
    sine = jnp.sin(angles)
    return (
        jnp.concatenate([cosine, cosine], axis=1),
        jnp.concatenate([-sine, sine], axis=1),
    )


def turn(block, cosine, sine):
    quarter = block.shape[-1] // 2
    swapped = jnp.concatenate([block[..., quarter:], block[..., :quarter]], axis=-1)
    return block * cosine + swapped * sine


def shift(values, by):
    size = lax.axis_size("fsdp")
    return lax.ppermute(values, "fsdp", [(i, (i + by) % size) for i in range(size)])


def gather_near(values):
    size = lax.axis_size("fsdp")
    return (
        lax.ppermute(values, "fsdp", [(i, i + 1) for i in range(size - 1)]),
        lax.ppermute(values, "fsdp", [(i + 1, i) for i in range(size - 1)]),
    )


def gather_far(values, near):
    size = lax.axis_size("fsdp")
    here = lax.axis_index("fsdp")
    above, below = near
    from_above, from_below = [values, above], [values, below]
    for k in range(2, size):
        links = [(i, i + k - 1) for i in range(1, size - k + 1)]
        from_above.append(lax.ppermute(above, "fsdp", links))
        links = [(size - 1 - i, size - 1 - j) for i, j in links]
        from_below.append(lax.ppermute(below, "fsdp", links))
    return [values] + [
        jnp.where(here >= k, from_above[k], from_below[size - k]) for k in range(1, size)
    ]


def gather_group(values):
    return gather_far(values, gather_near(values))


def send_home(blocks):
    return [blocks[0]] + [shift(blocks[k], -k) for k in range(1, len(blocks))]


def send_out(blocks):
    return [blocks[0]] + [shift(blocks[k], k) for k in range(1, len(blocks))]


def pick(choices, which):
    result = choices[0]
    for i in range(1, len(choices)):
        result = jnp.where(which == i, choices[i], result)
    return result


def split_rows(values, parts):
    rows = values.shape[0] // parts
    return [values[k * rows : (k + 1) * rows] for k in range(parts)]


def split_cols(values, parts):
    cols = values.shape[1] // parts
    return [values[:, k * cols : (k + 1) * cols] for k in range(parts)]


def add_up(pieces):
    total = pieces[0].astype(jnp.float32)
    for piece in pieces[1:]:
        total = total + piece.astype(jnp.float32)
    return total


def attention_mask(info_ref, count, slots):
    rows = lax.broadcasted_iota(jnp.int32, (count, count), 0)
    cols = lax.broadcasted_iota(jnp.int32, (count, count), 1)
    end_at = 0
    same = None
    for s in range(slots):
        end_at = end_at + info_ref[1 + s]
        agree = (rows >= end_at) == (cols >= end_at)
        same = agree if same is None else same & agree
    return same & (cols <= rows) & (rows - cols < WINDOW)


def cost(multiply_adds, read_and_written):
    return pl.CostEstimate(
        flops=2 * multiply_adds, bytes_accessed=read_and_written, transcendentals=0
    )


def mxu(left, right, left_dim, right_dim):
    return lax.dot_general(
        left, right, (((left_dim,), (right_dim,)), ((), ())), preferred_element_type=jnp.float32
    )


def soft(queries, keys, allowed):
    scores = jnp.where(allowed, mxu(queries, keys, 1, 1), NEG_BIG)
    raised = jnp.exp(scores - jnp.max(scores, axis=1, keepdims=True))
    return raised / jnp.sum(raised, axis=1, keepdims=True)


def forward_kernel(slots, q_cols, info_ref, *refs):
    size = len(refs) - 3
    came, (att_ref, q_ref, kv_ref) = refs[:size], refs[size:]
    here = info_ref[0]
    kv_cols = came[0].shape[1] - q_cols
    for k in range(size):
        at = lax.rem(here + k, size)
        q_ref[:, pl.ds(pl.multiple_of(at * q_cols, 128), q_cols)] = came[k][:, :q_cols]
        kv_ref[:, pl.ds(pl.multiple_of(at * kv_cols, 128), kv_cols)] = came[k][:, q_cols:]
    allowed = attention_mask(info_ref, q_ref.shape[0], slots)
    keys = kv_ref[:, :HD]
    values = kv_ref[:, HD:]
    for h in range(H):
        probs = soft(q_ref[:, h * HD : (h + 1) * HD], keys, allowed)
        att_ref[:, h * HD : (h + 1) * HD] = mxu(
            probs.astype(jnp.bfloat16), values, 1, 0
        ).astype(jnp.bfloat16)


def backward_kernel(slots, q_cols, info_ref, q_ref, kv_ref, cos_ref, sin_ref, *refs):
    parts, out_ref = refs[:-1], refs[-1]
    low = jnp.bfloat16
    half = HD // 2
    size = out_ref.shape[0]
    here = info_ref[0]
    allowed = attention_mask(info_ref, q_ref.shape[0], slots)
    keys = kv_ref[:, :HD]
    values = kv_ref[:, HD:]
    cosine = cos_ref[...]
    sine = sin_ref[...]
    kv_cols = out_ref.shape[2] - q_cols
    key_grad = jnp.zeros((q_ref.shape[0], HD), jnp.float32)
    value_grad = jnp.zeros((q_ref.shape[0], HD), jnp.float32)

    def back(block):
        swapped = jnp.concatenate([block[:, half // 2 :], block[:, : half // 2]], axis=1)
        return block * cosine - swapped * sine

    def place(block, column, width, offset):
        entry = lax.rem(column // width - here + size, size)
        start = offset + column % width
        out_ref[entry, :, start : start + half] = block.astype(low)

    for h in range(H):
        cols = slice(h * HD, (h + 1) * HD)
        queries = q_ref[:, cols]
        grads = parts[0][:, cols].astype(jnp.float32)
        for part in parts[1:]:
            grads = grads + part[:, cols].astype(jnp.float32)
        grads = grads.astype(low)
        probs = soft(queries, keys, allowed)
        grad_prob = mxu(grads, values, 1, 1)
        value_grad = value_grad + mxu(probs.astype(low), grads, 0, 0)
        row_delta = jnp.sum(probs * grad_prob, axis=1, keepdims=True)
        grad_score = (probs * (grad_prob - row_delta)).astype(low)
        key_grad = key_grad + mxu(grad_score, queries, 0, 0)
        query_grad = mxu(grad_score, keys, 1, 0) * HD ** (-0.5)
        place(back(query_grad[:, :half]), h * HD, q_cols, 0)
        place(query_grad[:, half:], h * HD + half, q_cols, 0)
    place(back(key_grad[:, :half]), 0, kv_cols, q_cols)
    place(key_grad[:, half:], half, kv_cols, q_cols)
    place(value_grad[:, :half], HD, kv_cols, q_cols)
    place(value_grad[:, half:], HD + half, kv_cols, q_cols)


def kernel_specs(count):
    return [pl.BlockSpec(memory_space=pltpu.SMEM)] + [
        pl.BlockSpec(memory_space=pltpu.VMEM)
    ] * count


def attend(info, came, q_cols):
    rows = came[0].shape[0]
    slots = info.shape[0] - 1
    return pl.pallas_call(
        functools.partial(forward_kernel, slots, q_cols),
        out_shape=(
            jax.ShapeDtypeStruct((rows, H * HD), jnp.bfloat16),
            jax.ShapeDtypeStruct((rows, H * HD), jnp.bfloat16),
            jax.ShapeDtypeStruct((rows, 2 * HD), jnp.bfloat16),
        ),
        in_specs=kernel_specs(len(came)),
        out_specs=(pl.BlockSpec(memory_space=pltpu.VMEM),) * 3,
        compiler_params=pltpu.CompilerParams(vmem_limit_bytes=32 * 2**20),
    )(info, *came)


def attend_back(info, queries, keys_values, cosine, sine, parts, q_cols, kv_cols):
    rows = queries.shape[0]
    slots = info.shape[0] - 1
    size = len(parts)
    return pl.pallas_call(
        functools.partial(backward_kernel, slots, q_cols),
        out_shape=jax.ShapeDtypeStruct((size, rows, q_cols + kv_cols), jnp.bfloat16),
        in_specs=kernel_specs(4 + size),
        out_specs=pl.BlockSpec(memory_space=pltpu.VMEM),
        compiler_params=pltpu.CompilerParams(vmem_limit_bytes=32 * 2**20),
    )(info, queries, keys_values, cosine, sine, *parts)


def spread_kernel(place_ref, left_a, right_a, left_b, right_b, keep_ref, send_ref):
    rows = keep_ref.shape[1]
    width = right_a.shape[1]
    chunk = 640
    for c in range(left_a.shape[1] // chunk):
        cols = slice(c * chunk, (c + 1) * chunk)
        full_a = mxu(left_a[:, cols], right_a[...], 0, 0).astype(jnp.bfloat16)
        full_b = mxu(left_b[:, cols], right_b[...], 0, 0).astype(jnp.bfloat16)
        for t in range(chunk // rows):
            entry = jnp.bitwise_xor(c * (chunk // rows) + t, place_ref[0])
            at = lax.div(entry, 2)
            even = entry - 2 * at == 0
            block_a = full_a[t * rows : (t + 1) * rows]
            block_b = full_b[t * rows : (t + 1) * rows]

            @pl.when(even)
            def _():
                keep_ref[at, :, :width] = block_a
                keep_ref[at, :, width:] = block_b

            @pl.when(jnp.logical_not(even))
            def _():
                send_ref[at, :, :width] = block_a
                send_ref[at, :, width:] = block_b


def spread_products(place, left_a, right_a, left_b, right_b, count):
    features = left_a.shape[1]
    width = right_a.shape[1] + right_b.shape[1]
    shape = jax.ShapeDtypeStruct((count // 2, features // count, width), jnp.bfloat16)
    return pl.pallas_call(
        spread_kernel,
        out_shape=(shape, shape),
        in_specs=kernel_specs(4),
        out_specs=(pl.BlockSpec(memory_space=pltpu.VMEM),) * 2,
        cost_estimate=cost(left_a.size * width, 2 * features * width),
        compiler_params=pltpu.CompilerParams(vmem_limit_bytes=48 * 2**20),
    )(place, left_a, right_a, left_b, right_b)


def swap(values, mask):
    count = lax.axis_size("dp")
    return lax.ppermute(values, "dp", [(i, i ^ mask) for i in range(count)])


def add_low(one, two):
    return (one.astype(jnp.float32) + two.astype(jnp.float32)).astype(jnp.bfloat16)


def halve(part, order, beside):
    left = sorted(order, reverse=True)
    for bit in order:
        axis = left.index(bit)
        cube = part.reshape((2,) * len(left) + part.shape[-2:])
        stay = lax.index_in_dim(cube, 0, axis, keepdims=False)
        leave = lax.index_in_dim(cube, 1, axis, keepdims=False)
        if len(left) == len(order) and beside is not None:
            stay, beside = lax.optimization_barrier((stay, beside))
        part = add_low(stay, swap(leave, 2 << bit))
        left.remove(bit)
    return part, beside


ROOT = (2.0 / math.pi) ** 0.5
CUBE = 0.044715


def add_up_blocks(total, part):
    step = pl.program_id(0)

    @pl.when(step == 0)
    def _():
        total[...] = part

    @pl.when(step > 0)
    def _():
        total[...] += part


def feed_forward_kernel(
    info_ref, normed_ref, gate_w, up_w, down_w, gate_ref, up_ref, hidden_ref, out_ref, total
):
    gate_lin = mxu(normed_ref[...], gate_w[...], 1, 0)
    up_lin = mxu(normed_ref[...], up_w[...], 1, 0)
    gate_ref[...] = gate_lin
    up_ref[...] = up_lin
    bend = jnp.tanh(ROOT * (gate_lin + CUBE * gate_lin * gate_lin * gate_lin))
    hidden = (0.5 * gate_lin * (1.0 + bend) * up_lin).astype(jnp.bfloat16)
    hidden_ref[...] = hidden
    add_up_blocks(total, mxu(hidden, down_w[...], 1, 1))

    @pl.when(pl.program_id(0) == pl.num_programs(0) - 1)
    def _():
        size, rows, _ = out_ref.shape
        for k in range(size):
            owner = lax.rem(info_ref[0] - k + size, size)
            out_ref[owner] = total[k * rows : (k + 1) * rows, :].astype(out_ref.dtype)


def feed_back_kernel(grad_ref, gate_lin, up_lin, down_w, gate_ref, lin_ref):
    hidden_grad = mxu(grad_ref[...], down_w[...], 1, 0)
    gate = gate_lin[...]
    square = gate * gate
    bend = jnp.tanh(ROOT * (gate + CUBE * square * gate))
    half = 0.5 * (1.0 + bend)
    slope = half + 0.5 * gate * (1.0 - bend * bend) * (ROOT * (1.0 + 3 * CUBE * square))
    gate_ref[...] = (hidden_grad * up_lin[...] * slope).astype(jnp.bfloat16)
    lin_ref[...] = (hidden_grad * (gate * half)).astype(jnp.bfloat16)


def back_product_kernel(gate_ref, lin_ref, gate_w, up_w, *out_refs):
    part = mxu(gate_ref[...], gate_w[...], 1, 1) + mxu(lin_ref[...], up_w[...], 1, 1)
    rows = part.shape[0] // len(out_refs)
    for k, out_ref in enumerate(out_refs):
        out_ref[...] = part[k * rows : (k + 1) * rows, :].astype(out_ref.dtype)


def unit_blocks(rows, weights):
    features, width = weights.shape
    units = width // 3
    step = 640 if units % 640 == 0 else 384
    steps = units // step
    whole = pl.BlockSpec((rows, features), lambda i: (0, 0), pipeline_mode=pl.Buffered(1))
    part = pl.BlockSpec((rows, step), lambda i: (0, i))
    blocks = [
        pl.BlockSpec((features, step), lambda i, at=at: (0, i + at * steps)) for at in range(3)
    ]
    return units, steps, whole, part, blocks


def feed_forward(info, normed, weights, size):
    rows, features = normed.shape
    units, steps, whole, part, blocks = unit_blocks(rows, weights)
    low = jnp.bfloat16
    result = pl.pallas_call(
        feed_forward_kernel,
        grid=(steps,),
        out_shape=(jax.ShapeDtypeStruct((rows, units), jnp.float32),) * 2
        + (
            jax.ShapeDtypeStruct((rows, units), low),
            pltpu.HBM((size, rows // size, 2 * features), low),
        ),
        in_specs=[pl.BlockSpec(memory_space=pltpu.SMEM), whole, *blocks],
        out_specs=(part,) * 3
        + (pl.BlockSpec((size, rows // size, features), lambda i: (0, 0, 0)),),
        scratch_shapes=[pltpu.VMEM((rows, features), jnp.float32)],
        cost_estimate=cost(3 * rows * features * units, 2 * weights.size + 14 * rows * units),
        compiler_params=pltpu.CompilerParams(vmem_limit_bytes=58 * 2**20),
    )(info, normed, weights, weights, weights)
    return result


def feed_back(grads, gate_lin, up_lin, weights):
    rows, features = grads.shape
    units, steps, whole, part, blocks = unit_blocks(rows, weights)
    return pl.pallas_call(
        feed_back_kernel,
        grid=(steps,),
        out_shape=(jax.ShapeDtypeStruct((rows, units), jnp.bfloat16),) * 2,
        in_specs=[whole, part, part, blocks[2]],
        out_specs=(part,) * 2,
        cost_estimate=cost(rows * features * units, 2 * features * units + 12 * rows * units),
        compiler_params=pltpu.CompilerParams(vmem_limit_bytes=58 * 2**20),
    )(grads, gate_lin, up_lin, weights)


def back_product(gate_low, lin_low, weights, half, size):
    rows, units = gate_low.shape
    features = weights.shape[0] // 2
    step = 640
    start = half * (features // step)
    whole = pl.BlockSpec((rows, units), lambda i: (0, 0), pipeline_mode=pl.Buffered(1))
    return list(
        pl.pallas_call(
            back_product_kernel,
            grid=(features // step,),
            out_shape=(jax.ShapeDtypeStruct((rows // size, features), jnp.bfloat16),) * size,
            in_specs=[
                whole,
                whole,
                pl.BlockSpec((step, units), lambda i: (i + start, 0)),
                pl.BlockSpec((step, units), lambda i: (i + start, 1)),
            ],
            out_specs=(pl.BlockSpec((rows // size, step), lambda i: (0, i)),) * size,
            cost_estimate=cost(2 * rows * features * units, 4 * features * units),
            compiler_params=pltpu.CompilerParams(vmem_limit_bytes=58 * 2**20),
        )(gate_low, lin_low, weights, weights)
    )


def last_product_kernel(info_ref, grad_ref, w_ref, token_ref, inverse_ref, _, out_ref, gain_ref):
    part = mxu(grad_ref[...], w_ref[...], 1, 1)
    scaled = part * (token_ref[...].astype(jnp.float32) * inverse_ref[...])
    gain_ref[...] = jnp.sum(scaled, axis=0, keepdims=True)
    size, rows, _ = out_ref.shape
    for k in range(size):
        owner = lax.rem(info_ref[0] - k + size, size)
        out_ref[owner] = part[k * rows : (k + 1) * rows, :].astype(out_ref.dtype)


def last_product(info, grads, weights, tokens, inverse, wide):
    rows, features = tokens.shape
    step = 640
    start = features // step
    size = wide.shape[0]
    return pl.pallas_call(
        last_product_kernel,
        grid=(features // step,),
        out_shape=(
            pltpu.HBM(wide.shape, wide.dtype),
            jax.ShapeDtypeStruct((1, features), jnp.float32),
        ),
        in_specs=[
            pl.BlockSpec(memory_space=pltpu.SMEM),
            pl.BlockSpec(grads.shape, lambda i: (0, 0)),
            pl.BlockSpec((step, grads.shape[1]), lambda i: (i, 0)),
            pl.BlockSpec((rows, step), lambda i: (0, i)),
            pl.BlockSpec((rows, 1), lambda i: (0, 0)),
            pl.BlockSpec(memory_space=pltpu.HBM),
        ],
        out_specs=(
            pl.BlockSpec((size, rows // size, step), lambda i: (0, 0, i + start)),
            pl.BlockSpec((1, step), lambda i: (0, i)),
        ),
        input_output_aliases={5: 0},
        cost_estimate=cost(rows * features * grads.shape[1], 6 * rows * features),
        compiler_params=pltpu.CompilerParams(vmem_limit_bytes=32 * 2**20),
    )(info, grads, weights, tokens, inverse, wide)


def product_kernel(left_ref, *refs):
    out_ref = refs[-1]
    start = 0
    for right_ref in refs[:-1]:
        width = right_ref.shape[1]
        out_ref[:, start : start + width] = mxu(left_ref[...], right_ref[...], 0, 0).astype(
            out_ref.dtype
        )
        start += width


def product(left, *rights):
    rows, features = left.shape
    step = 640
    width = sum(right.shape[1] for right in rights)
    return pl.pallas_call(
        product_kernel,
        grid=(features // step,),
        out_shape=jax.ShapeDtypeStruct((features, width), jnp.bfloat16),
        in_specs=[pl.BlockSpec((rows, step), lambda i: (0, i))]
        + [
            pl.BlockSpec(right.shape, lambda i: (0, 0), pipeline_mode=pl.Buffered(1))
            for right in rights
        ],
        out_specs=pl.BlockSpec((step, width), lambda i: (i, 0)),
        cost_estimate=cost(rows * features * width, 2 * features * width),
        compiler_params=pltpu.CompilerParams(vmem_limit_bytes=58 * 2**20),
    )(left, *rights)


def update_kernel(rates, factor_ref, o_ref, qkv_ref, up_ref, down_ref, *refs):
    count = len(rates)
    factor = factor_ref[0, 0]
    sources = (o_ref, qkv_ref, qkv_ref, up_ref, down_ref)
    start = 0
    for m in range(count):
        first, second, weight = refs[m], refs[count + m], refs[2 * count + m]
        outs = refs[3 * count + 5 * m : 3 * count + 5 * (m + 1)]
        parts = [()] if len(weight.shape) == 2 else [(p,) for p in range(weight.shape[0])]
        width = weight.shape[-1]
        if m == 0 or sources[m] is not sources[m - 1]:
            start = 0
        for part in parts:
            gradient = sources[m][:, start : start + width].astype(jnp.float32)
            start += width
            results = adamw(
                gradient, first[part + (...,)], second[part + (...,)], weight[part + (...,)],
                factor, rates[m],
            )
            for out, result in zip(outs, results):
                out[part + (...,)] = result


def update(factor, gradients, masters, firsts, seconds, rates):
    rows = gradients[0].shape[0]
    step = 32 if rows % 32 == 0 else 16

    def spec(shape):
        if len(shape) == 2:
            return pl.BlockSpec((step, shape[1]), lambda i: (i, 0))
        return pl.BlockSpec((shape[0], step, shape[2]), lambda i: (0, i, 0))

    states = (*firsts, *seconds, *masters)
    out_shape, out_specs = [], []
    for master in masters:
        for kind in (jnp.float32,) * 4 + (jnp.bfloat16,):
            out_shape.append(jax.ShapeDtypeStruct(master.shape, kind))
            out_specs.append(spec(master.shape))
    result = pl.pallas_call(
        functools.partial(update_kernel, rates),
        grid=(rows // step,),
        out_shape=out_shape,
        in_specs=[pl.BlockSpec(memory_space=pltpu.SMEM)]
        + [spec(g.shape) for g in gradients]
        + [spec(one.shape) for one in states],
        out_specs=out_specs,
        cost_estimate=cost(0, sum(10 * m.size for m in states)),
        compiler_params=pltpu.CompilerParams(vmem_limit_bytes=58 * 2**20),
    )(factor.reshape(1, 1), *gradients, *states)
    return [result[5 * m : 5 * m + 5] for m in range(len(masters))]


def sum_along(axis, values):
    size = lax.axis_size(axis)
    step = 1
    while step < size:
        values = values + lax.ppermute(values, axis, [(i, i ^ step) for i in range(size)])
        step *= 2
    return values


def sum_everywhere(values):
    return sum_along("dp", sum_along("fsdp", values))


def adamw(gradient, first_mom, second_mom, weight, factor, step_rate):
    clipped = gradient * factor
    first_new = BETA_ONE * first_mom + (1.0 - BETA_ONE) * clipped
    second_new = BETA_TWO * second_mom + (1.0 - BETA_TWO) * clipped * clipped
    first_hat = first_new / (1.0 - BETA_ONE**STEP)
    second_hat = second_new / (1.0 - BETA_TWO**STEP)
    weight_new = weight - step_rate * (
        first_hat / (jnp.sqrt(second_hat) + EPS_ADAM) + DECAY_RATE * weight
    )
    return (clipped, first_new, second_new, weight_new, weight_new.astype(jnp.bfloat16))


def body(
    tokens,
    cotangent,
    seq_lengths,
    wq_master,
    wkv_master,
    wo_master,
    ffw_up_master,
    ffw_down_master,
    vec_master,
    wq_first,
    wq_second,
    wkv_first,
    wkv_second,
    wo_first,
    wo_second,
    ffw_up_first,
    ffw_up_second,
    ffw_down_first,
    ffw_down_second,
    vec_first,
    vec_second,
):
    size = lax.axis_size("fsdp")
    here = lax.axis_index("fsdp")
    owner = lax.axis_index("dp") * size + here
    tok_count = tokens.shape[0]
    vec_cols = vec_master.shape[1]
    q_cols = wq_master.shape[1]
    kv_cols = wkv_master.shape[1]
    low = jnp.bfloat16
    contract_rows = (((0,), (0,)), ((), ()))
    contract_cols = (((1,), (1,)), ((), ()))

    def dot(left, right):
        return jnp.dot(left, right, preferred_element_type=jnp.float32)

    def dot_rows(left, right):
        return lax.dot_general(left, right, contract_rows, preferred_element_type=jnp.float32)

    def dot_cols(left, right):
        return lax.dot_general(left, right, contract_cols, preferred_element_type=jnp.float32)

    attn_weights = lax.all_gather(
        jnp.concatenate([wq_master, wkv_master, wo_master], axis=1).astype(low),
        "dp",
        axis=0,
        tiled=True,
    )
    units = ffw_up_master.shape[2]
    qkv_full = attn_weights[:, : q_cols + kv_cols]
    wo_cols = attn_weights[:, q_cols + kv_cols :]

    token_near = gather_near(tokens)

    slots = seq_lengths.shape[1]
    small = jnp.zeros((8, 128), jnp.float32)
    small = lax.dynamic_update_slice(small, vec_master.astype(low).astype(jnp.float32), (0, 0))
    small = lax.dynamic_update_slice(small, seq_lengths.astype(jnp.float32), (4, 0))
    small_blocks = [small] + [shift(small, k) for k in range(1, size)]
    length_blocks = [b[4, :slots].astype(jnp.int32) for b in small_blocks]
    vec_low = jnp.zeros((4, D), jnp.float32)
    for k in range(size):
        block_at = owner - here + (here - k) % size
        vec_low = lax.dynamic_update_slice(
            vec_low, small_blocks[k][:4, :vec_cols], (0, block_at * vec_cols)
        )
    up_master, down_master, vec_low = lax.optimization_barrier(
        (ffw_up_master, ffw_down_master, vec_low)
    )
    ffw_shard = jnp.concatenate(
        [up_master[0].astype(low), up_master[1].astype(low), down_master.T.astype(low)], axis=1
    )
    vec_low = sum_along("dp", vec_low)
    vec_low, token_near, ffw_shard = lax.optimization_barrier((vec_low, token_near, ffw_shard))
    ffw_weights = lax.all_gather(ffw_shard, "dp", axis=0, tiled=True)

    token_blocks = gather_far(tokens, token_near)
    gain_one, bias_one, gain_two, bias_two = (vec_low[i : i + 1] for i in range(4))
    group_tokens = jnp.concatenate(token_blocks, axis=0)
    places, segment, position, valid_mask = layout(seq_lengths[0], tok_count)
    valid_col = valid_mask[:, None]
    group_position = jnp.concatenate([layout(b, tok_count)[2] for b in length_blocks])
    grad_out = cotangent.astype(jnp.float32) * valid_col
    grad_low, group_tokens = lax.optimization_barrier((grad_out.astype(low), group_tokens))
    grad_near = gather_near(grad_low)
    x_group = group_tokens.astype(jnp.float32)
    group_inverse = lax.rsqrt(jnp.mean(x_group * x_group, axis=1, keepdims=True) + EPS_NORM)
    normed = (x_group * group_inverse * gain_one).astype(low)
    qkv_lin = dot(normed, qkv_full)
    group_cos, group_sin = angle_tables(group_position)
    half_dim = HD // 2
    turned = []
    for b in range((q_cols + kv_cols) // half_dim):
        block = qkv_lin[:, b * half_dim : (b + 1) * half_dim]
        if b * half_dim < q_cols:
            rotated = (here * (q_cols // half_dim) + b) % 2 == 0
            scale = HD ** (-0.5)
        else:
            rotated = here * (kv_cols // half_dim) + b - q_cols // half_dim == 0
            scale = 1.0
        turned.append((jnp.where(rotated, turn(block, group_cos, group_sin), block) * scale).astype(low))
    qkv_low = jnp.concatenate(turned, axis=1)
    came = send_home(split_rows(qkv_low, size))
    came, grad_near = lax.optimization_barrier((came, grad_near))

    def in_order(pieces):
        return jnp.concatenate([pick(pieces, (j - here) % size) for j in range(size)], axis=1)

    info = jnp.concatenate([here.astype(jnp.int32)[None], seq_lengths[0]])
    attended, queries, keys_values = attend(info, came, q_cols)
    group_attended = jnp.concatenate(gather_group(attended), axis=0)
    branch = dot(group_attended, wo_cols).astype(low)
    branch = in_order(send_home(split_rows(branch, size))).astype(jnp.float32)
    x_float = tokens.astype(jnp.float32)
    inverse = group_inverse[:tok_count]
    mixed = x_float + valid_col * (branch + bias_one)
    inv_two = lax.rsqrt(jnp.mean(mixed * mixed, axis=1, keepdims=True) + EPS_NORM)
    normed_two = (mixed * inv_two * gain_two).astype(low)
    group_normed = jnp.concatenate(gather_group(normed_two), axis=0)

    grad_near, group_normed, ffw_weights = lax.optimization_barrier(
        (grad_near, group_normed, ffw_weights)
    )
    group_grad = jnp.concatenate(gather_far(grad_low, grad_near), axis=0)

    gate_lin, up_lin, hidden, ffw_part = feed_forward(info, group_normed, ffw_weights, size)
    group_grad, ffw_part = lax.optimization_barrier((group_grad, ffw_part))
    down_grad = product(group_grad, hidden)
    own_down = lax.psum_scatter(down_grad, "dp", scatter_dimension=0, tiled=True)
    group_grad, down_grad = lax.optimization_barrier((group_grad, down_grad))
    gate_low, lin_low = feed_back(group_grad, gate_lin, up_lin, ffw_weights)
    first_pieces = send_home(back_product(gate_low, lin_low, ffw_weights, 0, size))
    second_pieces = send_home(back_product(gate_low, lin_low, ffw_weights, 1, size))
    gate_last, first_pieces = lax.optimization_barrier((gate_low, first_pieces))
    up_grad = product(group_normed, gate_last, lin_low)
    up_grad, second_pieces = lax.optimization_barrier((up_grad, second_pieces))
    normed_two_grad = jnp.concatenate([add_up(first_pieces), add_up(second_pieces)], axis=1)
    own_up = lax.psum_scatter(up_grad, "dp", scatter_dimension=0, tiled=True)
    bias_two_grad = jnp.sum(grad_out, axis=0)

    gain_two_grad = jnp.sum(normed_two_grad * mixed * inv_two, axis=0)
    scaled_two = normed_two_grad * gain_two
    mixed_grad = (
        inv_two
        * (
            scaled_two
            - mixed * inv_two * inv_two * jnp.mean(scaled_two * mixed, axis=1, keepdims=True)
        )
        + grad_out
    )
    branch_low = (mixed_grad * valid_col).astype(low)
    bias_one_grad = jnp.sum(branch_low.astype(jnp.float32), axis=0)

    def column_blocks(values):
        blocks = split_cols(values, size)
        return [pick(blocks, (here + k) % size) for k in range(size)]

    branch_cols = jnp.concatenate(send_out(column_blocks(branch_low)), axis=0)
    attn_part = dot_cols(branch_cols, wo_cols).astype(low)
    place = lax.axis_index("dp").astype(jnp.int32)[None]
    dp_size = lax.axis_size("dp")
    attn_pieces = send_home(split_rows(attn_part, size))
    outgoing = attend_back(
        info,
        queries,
        keys_values,
        group_cos[:tok_count],
        group_sin[:tok_count],
        attn_pieces,
        q_cols,
        kv_cols,
    )
    qkv_grad = jnp.concatenate(send_out([outgoing[k] for k in range(size)]), axis=0)
    keep, send = spread_products(place, group_attended, branch_cols, normed, qkv_grad, dp_size)
    got = swap(send, 1)
    wide, gain_one_grad = last_product(
        info, qkv_grad, attn_weights, group_tokens, group_inverse, ffw_part
    )
    wide, got = lax.optimization_barrier((wide, got))
    last_sums = lax.psum_scatter(
        wide.reshape(size * tok_count, 2 * D), "fsdp", scatter_dimension=0, tiled=True
    )

    def square_sum(values):
        values = values.astype(jnp.float32)
        return jnp.sum(values * values)

    ffw_squares = square_sum(own_down) + square_sum(own_up)
    total = add_low(keep, got)
    bits = list(range(keep.shape[0].bit_length() - 1))
    own_o, _ = halve(total[:, :, :q_cols], bits, ffw_squares)
    own_qkv, ffw_squares = halve(total[:, :, q_cols:], bits[::-1], ffw_squares)
    vec_grad = sum_everywhere(
        jnp.stack([gain_one_grad[0], bias_one_grad, gain_two_grad, bias_two_grad])
    )
    def square_sum(values):
        values = values.astype(jnp.float32)
        return jnp.sum(values * values)

    squares = square_sum(own_down) + square_sum(own_up)
    own_vec = lax.dynamic_slice(vec_grad, (0, owner * vec_cols), (4, vec_cols))

    squares = ffw_squares + square_sum(own_o) + square_sum(own_qkv)
    squares = sum_along("fsdp", sum_along("dp", jnp.broadcast_to(squares, (8, 128))))[0, 0]
    grad_norm = jnp.sqrt(squares + jnp.sum(vec_grad * vec_grad))
    factor = jnp.minimum(1.0, CLIP_NORM / grad_norm)
    o_out, q_out, kv_out, up_out, down_out = update(
        factor,
        (own_o, own_qkv, own_up, own_down),
        (wo_master, wq_master, wkv_master, ffw_up_master, ffw_down_master.T),
        (wo_first, wq_first, wkv_first, ffw_up_first, ffw_down_first.T),
        (wo_second, wq_second, wkv_second, ffw_up_second, ffw_down_second.T),
        ((H * HD // 32) ** (-0.5), D ** (-0.5), D ** (-0.5), D ** (-0.5), FF ** (-0.5)),
    )
    last_sums, down_out = lax.optimization_barrier((last_sums, down_out))
    ffw_term = last_sums[:, :D].astype(jnp.float32)
    block_out = (mixed + valid_col * (ffw_term + bias_two)).astype(low)
    normed_grad = last_sums[:, D:]
    scaled = normed_grad.astype(jnp.float32) * gain_one
    input_grad = (
        inverse
        * (scaled - x_float * inverse * inverse * jnp.mean(scaled * x_float, axis=1, keepdims=True))
        + mixed_grad
    ).astype(low)
    down_out = [one.T for one in down_out]
    vec_out = adamw(own_vec, vec_first, vec_second, vec_master, factor, LR_VECTOR)
    return (
        block_out,
        input_grad,
        grad_norm,
        q_out[0],
        q_out[1],
        q_out[2],
        q_out[3],
        q_out[4],
        kv_out[0],
        kv_out[1],
        kv_out[2],
        kv_out[3],
        kv_out[4],
        o_out[0],
        o_out[1],
        o_out[2],
        o_out[3],
        o_out[4],
        up_out[0],
        up_out[1],
        up_out[2],
        up_out[3],
        up_out[4],
        down_out[0],
        down_out[1],
        down_out[2],
        down_out[3],
        down_out[4],
        vec_out[0],
        vec_out[1],
        vec_out[2],
        vec_out[3],
        vec_out[4],
    )


def solution(mesh):
    placed = (
        P(("dp", "fsdp"), None),
        P(("dp", "fsdp"), None),
        P(("dp", "fsdp"), None),
        P("dp", "fsdp"),
        P("dp", "fsdp"),
        P("dp", "fsdp"),
        P(None, "dp", "fsdp"),
        P("fsdp", "dp"),
        P(None, ("dp", "fsdp")),
        P("dp", "fsdp"),
        P("dp", "fsdp"),
        P("dp", "fsdp"),
        P("dp", "fsdp"),
        P("dp", "fsdp"),
        P("dp", "fsdp"),
        P(None, "dp", "fsdp"),
        P(None, "dp", "fsdp"),
        P("fsdp", "dp"),
        P("fsdp", "dp"),
        P(None, ("dp", "fsdp")),
        P(None, ("dp", "fsdp")),
    )
    return jax.shard_map(
        body,
        mesh=mesh,
        in_specs=placed,
        out_specs=(
            P(("dp", "fsdp"), None),
            P(("dp", "fsdp"), None),
            P(),
            P("dp", "fsdp"),
            P("dp", "fsdp"),
            P("dp", "fsdp"),
            P("dp", "fsdp"),
            P("dp", "fsdp"),
            P("dp", "fsdp"),
            P("dp", "fsdp"),
            P("dp", "fsdp"),
            P("dp", "fsdp"),
            P("dp", "fsdp"),
            P("dp", "fsdp"),
            P("dp", "fsdp"),
            P("dp", "fsdp"),
            P("dp", "fsdp"),
            P("dp", "fsdp"),
            P(None, "dp", "fsdp"),
            P(None, "dp", "fsdp"),
            P(None, "dp", "fsdp"),
            P(None, "dp", "fsdp"),
            P(None, "dp", "fsdp"),
            P("fsdp", "dp"),
            P("fsdp", "dp"),
            P("fsdp", "dp"),
            P("fsdp", "dp"),
            P("fsdp", "dp"),
            P(None, ("dp", "fsdp")),
            P(None, ("dp", "fsdp")),
            P(None, ("dp", "fsdp")),
            P(None, ("dp", "fsdp")),
            P(None, ("dp", "fsdp")),
        ),
        check_vma=False,
    )
```

time: 1790 us -> 636 us (0.36)
  waiting for transfers between devices: 1360 us -> 268 us
  Pallas kernels: 0 us -> 144 us
  matrix products: 147 us -> 14.7 us
  blocking collectives: 120 us -> 0 us
  starting transfers between devices: 1.79 us -> 110 us
  other arithmetic: 102 us -> 56.8 us
    all_gather x9 -> x2, waiting for transfers between devices: 758 us -> 0.01 us  [the longest x1 0.01 us: body(): ffw_weights = lax.all_gather(ffw_shard, 'dp', axis=0, tiled=True)]
    reduce_scatter x10 -> x3, waiting for transfers between devices: 606 us -> 0.01 us  [the longest x1 0.01 us: body(): lax.psum_scatter(down_grad, 'dp', scatter_dimension=0, tiled=True)]
    ppermute x0 -> x66, waiting for transfers between devices: none -> 268 us  [the longest x24 113 us: shift(): lax.ppermute(values, 'fsdp', [(i, (i + by) % size) for i in range(size)])]
    pallas_call x0 -> x11, Pallas kernels: none -> 144 us  [the longest x1 28.8 us: feed_forward(): pl.pallas_call(feed_forward_kernel, grid=(steps,), out_shape=(jax.ShapeDt...]
    dot_general x24 -> x3, matrix products: 147 us -> 14.7 us  [the longest x2 9.9 us: dot(): return jnp.dot(left, right, preferred_element_type=jnp.float32)]
    ppermute x0 -> x66, starting transfers between devices: none -> 110 us  [the longest x24 49.6 us: shift(): lax.ppermute(values, 'fsdp', [(i, (i + by) % size) for i in range(size)])]
    all_gather x3 -> x0, blocking collectives: 45.1 us -> none  [the longest x1 23.7 us: body(): lax.all_gather(gathered[5], 'fsdp', axis=2, tiled=True)]
    psum x1 -> x0, blocking collectives: 40.5 us -> none  [body(): total_squares = lax.psum(local_squares, ('dp', 'fsdp'))]
  transfers between devices with their start and end apart: 19 -> 71, of which waited for: 19 -> 33; matrix products, arithmetic and copies ran while one was open for 9% -> 11% of each run, Pallas kernels for 0% -> 22%
where the time goes in v1:
time: 636 us; the launch traced here: 626 us
  waiting for transfers between devices  268 us (42%)
  Pallas kernels  144 us (23%)
  starting transfers between devices  110 us (17%)
  other arithmetic  56.8 us (9%)
  between operations  21.1 us (3%)
  matrix products  14.7 us (2%)
  local copies, waits for them, and re-layouts  11.4 us (2%)
    ppermute x24, waiting for transfers between devices, shift(): lax.ppermute(values, 'fsdp', [(i, (i + by) % size) for i in range(size)])  113 us
    ppermute x8, waiting for transfers between devices, gather_far(): from_below.append(lax.ppermute(below, 'fsdp', links))  91.8 us
    ppermute x24, starting transfers between devices, shift(): lax.ppermute(values, 'fsdp', [(i, (i + by) % size) for i in range(size)])  49.6 us
    pallas_call x1, Pallas kernels, feed_forward(): pl.pallas_call(feed_forward_kernel, grid=(steps,), out_shape=(jax.ShapeDt...  28.8 us
    pallas_call x1, Pallas kernels, update(): pl.pallas_call(functools.partial(update_kernel, rates), grid=(rows // ste...  28.1 us
    ppermute x4, waiting for transfers between devices, gather_near(): lax.ppermute(values, 'fsdp', [(i + 1, i) for i in range(size - 1)])  26.4 us
    pallas_call x2, Pallas kernels, product(): pl.pallas_call(product_kernel, grid=(features // step,), out_shape=jax.Sh...  25.9 us
    pallas_call x2, Pallas kernels, back_product(): pl.pallas_call(back_product_kernel, grid=(features // step,), out_shape=(...  23.6 us
  transfers between devices with their start and end apart: 71, of which 33 were waited for; matrix products, arithmetic and copies ran while one was open for 11% of the time, Pallas kernels for 22%

profile of v1, /device:TPU:0, one launch (start us, length us, event | category | flops | bytes accessed | tf_op | source)
XLA Modules:
  0.0 625.8 jit_solution(7281285333603467657)
XLA Ops:
  11.4 5.1 collective-permute-start.2
  17.5 5.2 collective-permute-start.6
  29.8 3.4 collective-permute-done.4
  51.1 29.0 %collective-permute-done.8 = bf16[128,2560]{1,0:T(8,128)(2,1)S(1)} collective-permute-done((bf16[128,2560]{1,0:T(8,128)(2,1)}, bf16[128,2560]{1,0:T(8,128)(2,1)S(1)}, u32[]{:S(2)}, u32[]{:S(2)}) %collective-permute-start.8) | collective-permute-done | bytes 655392 | tf_op jit(solution)/shard_map/ppermute | solution.py:82
  81.8 5.4 collective-permute-start.15
  90.0 5.1 fusion.3
  101.9 5.8 collective-permute-done.14.refs_3_
  107.7 4.8 collective-permute-done.13.refs_2_
  115.5 6.8 %collective-permute-start.17 = (bf16[128,2560]{1,0:T(8,128)(2,1)S(1)}, bf16[128,2560]{1,0:T(8,128)(2,1)S(1)}, u32[]{:S(2)}, u32[]{:S(2)}) collective-permute-start(bf16[128,2560]{1,0:T(8,128)(2,1)S(1)} %get-tuple-element.134), channel_id=1, source_target_pairs={{0,1},{1,2},{2,3},{4,5},{5,6},{6,7},{8,9},{9,10},{10,11},{12,13},{... | collective-permute-start | bytes 1966088 | tf_op jit(solution)/shard_map/ppermute | solution.py:68
  122.4 11.7 %collective-permute-done.18 = bf16[128,2560]{1,0:T(8,128)(2,1)S(1)} collective-permute-done((bf16[128,2560]{1,0:T(8,128)(2,1)S(1)}, bf16[128,2560]{1,0:T(8,128)(2,1)S(1)}, u32[]{:S(2)}, u32[]{:S(2)}) %collective-permute-start.18) | collective-permute-done | bytes 655392 | tf_op jit(solution)/shard_map/ppermute | solution.py:69
  138.1 16.4 %collective-permute-done.19 = bf16[128,2560]{1,0:T(8,128)(2,1)S(1)} collective-permute-done((bf16[128,2560]{1,0:T(8,128)(2,1)S(1)}, bf16[128,2560]{1,0:T(8,128)(2,1)S(1)}, u32[]{:S(2)}, u32[]{:S(2)}) %collective-permute-start.19) | collective-permute-done | bytes 655392 | tf_op jit(solution)/shard_map/ppermute | solution.py:82
  154.7 11.5 %collective-permute-done.21 = bf16[128,2560]{1,0:T(8,128)(2,1)S(1)} collective-permute-done((bf16[128,2560]{1,0:T(8,128)(2,1)S(1)}, bf16[128,2560]{1,0:T(8,128)(2,1)S(1)}, u32[]{:S(2)}, u32[]{:S(2)}) %collective-permute-start.21) | collective-permute-done | bytes 655392 | tf_op jit(solution)/shard_map/ppermute | solution.py:82
  166.3 4.8 fusion.8
  172.2 3.9 collective-permute-start.25
  177.2 3.8 collective-permute-done.25
  181.1 8.8 %collective-permute-done.24 = bf16[128,640]{1,0:T(8,128)(2,1)} collective-permute-done((bf16[128,640]{1,0:T(8,128)(2,1)}, bf16[128,640]{1,0:T(8,128)(2,1)}, u32[]{:S(2)}, u32[]{:S(2)}) %collective-permute-start.24) | collective-permute-done | bytes 163872 | tf_op jit(solution)/shard_map/ppermute | solution.py:62
  193.4 4.6 collective-permute-start.26
  198.0 12.0 %collective-permute-done.27 = bf16[128,2560]{1,0:T(8,128)(2,1)S(1)} collective-permute-done((bf16[128,2560]{1,0:T(8,128)(2,1)S(1)}, bf16[128,2560]{1,0:T(8,128)(2,1)S(1)}, u32[]{:S(2)}, u32[]{:S(2)}) %collective-permute-start.27) | collective-permute-done | bytes 655392 | tf_op jit(solution)/shard_map/ppermute | solution.py:69
  214.0 16.4 %collective-permute-done.28 = bf16[128,2560]{1,0:T(8,128)(2,1)S(1)} collective-permute-done((bf16[128,2560]{1,0:T(8,128)(2,1)S(1)}, bf16[128,2560]{1,0:T(8,128)(2,1)S(1)}, u32[]{:S(2)}, u32[]{:S(2)}) %collective-permute-start.28) | collective-permute-done | bytes 655392 | tf_op jit(solution)/shard_map/ppermute | solution.py:82
  230.6 11.3 %collective-permute-done.30 = bf16[128,2560]{1,0:T(8,128)(2,1)S(1)} collective-permute-done((bf16[128,2560]{1,0:T(8,128)(2,1)S(1)}, bf16[128,2560]{1,0:T(8,128)(2,1)S(1)}, u32[]{:S(2)}, u32[]{:S(2)}) %collective-permute-start.30) | collective-permute-done | bytes 655392 | tf_op jit(solution)/shard_map/ppermute | solution.py:82
  247.7 28.8 %shard_map.461 = (f32[512,1920]{1,0:T(8,128)}, f32[512,1920]{1,0:T(8,128)}, bf16[512,1920]{1,0:T(8,128)(2,1)}, bf16[4,128,5120]{2,1,0:T(8,128)(2,1)}) custom-call(s32[3]{0:T(128)} %copy-done.4, bf16[512,2560]{1,0:T(8,128)(2,1)} %pad_maximum_fusion.3.normed_ref.left_ref, bf16[2560,5760]{1,0:T(8,128)(2,1)} %all-gather.5.cloned.1.call-done.gate_w.up_w.down_w, ...), custom_call_target="tpu_custom_call" | custom-call | flops 15099494400 | bytes 43253760 | tf_op jit(solution)/shard_map/pallas_call | solution.py:388
  277.6 7.2 %collective-permute-done.32 = bf16[128,2560]{1,0:T(8,128)(2,1)S(1)} collective-permute-done((bf16[128,2560]{1,0:T(8,128)(2,1)}, bf16[128,2560]{1,0:T(8,128)(2,1)S(1)}, u32[]{:S(2)}, u32[]{:S(2)}) %collective-permute-start.32) | collective-permute-done | bytes 655392 | tf_op jit(solution)/shard_map/ppermute | solution.py:82
  287.5 9.5 %shard_map.462 = bf16[2560,1920]{1,0:T(8,128)(2,1)} custom-call(bf16[512,2560]{1,0:T(8,128)(2,1)} %pad_maximum_fusion.4.left_ref.grad_ref, bf16[512,1920]{1,0:T(8,128)(2,1)} %get-tuple-element.146.refs_0_), custom_call_target="tpu_custom_call" | custom-call | flops 5033164800 | bytes 9830400 | tf_op jit(solution)/shard_map/pallas_call | solution.py:499
  297.2 15.1 %shard_map.463 = (bf16[512,1920]{1,0:T(8,128)(2,1)}, bf16[512,1920]{1,0:T(8,128)(2,1)}) custom-call(bf16[512,2560]{1,0:T(8,128)(2,1)} %pad_maximum_fusion.4.left_ref.grad_ref, f32[512,1920]{1,0:T(8,128)} %get-tuple-element.148.gate_lin, f32[512,1920]{1,0:T(8,128)} %get-tuple-element.149.up_lin, bf16[2560,5760]{1,0:T(8,128)(2,1)} %all-gather.5.cloned.1.call-done.gate_w.up_w.down_w), custom_call_target="tpu_custom_call" | custom-call | flops 5033164800 | bytes 21626880 | tf_op jit(solution)/shard_map/pallas_call | solution.py:409
  312.3 12.1 %shard_map.464 = (bf16[128,1280]{1,0:T(8,128)(2,1)}, bf16[128,1280]{1,0:T(8,128)(2,1)}, bf16[128,1280]{1,0:T(8,128)(2,1)}, bf16[128,1280]{1,0:T(8,128)(2,1)}) custom-call(bf16[512,1920]{1,0:T(8,128)(2,1)} %get-tuple-element.160.gate_ref.refs_0_, bf16[512,1920]{1,0:T(8,128)(2,1)} %get-tuple-element.151.lin_ref.refs_1_, ...), custom_call_target="tpu_custom_call" | custom-call | flops 5033164800 | bytes 9830400 | tf_op jit(solution)/shard_map/pallas_call | solution.py:427
  324.4 3.8 collective-permute-start.37
  330.1 11.5 %shard_map.466 = (bf16[128,1280]{1,0:T(8,128)(2,1)}, bf16[128,1280]{1,0:T(8,128)(2,1)}, bf16[128,1280]{1,0:T(8,128)(2,1)}, bf16[128,1280]{1,0:T(8,128)(2,1)}) custom-call(bf16[512,1920]{1,0:T(8,128)(2,1)} %get-tuple-element.160.gate_ref.refs_0_, bf16[512,1920]{1,0:T(8,128)(2,1)} %get-tuple-element.151.lin_ref.refs_1_, ...), custom_call_target="tpu_custom_call" | custom-call | flops 5033164800 | bytes 9830400 | tf_op jit(solution)/shard_map/pallas_call | solution.py:427
  344.2 15.1 %collective-permute-done.37 = bf16[128,1280]{1,0:T(8,128)(2,1)} collective-permute-done((bf16[128,1280]{1,0:T(8,128)(2,1)}, bf16[128,1280]{1,0:T(8,128)(2,1)}, u32[]{:S(2)}, u32[]{:S(2)}) %collective-permute-start.37) | collective-permute-done | bytes 327712 | tf_op jit(solution)/shard_map/ppermute | solution.py:62
  359.3 16.4 %shard_map.465 = bf16[2560,3840]{1,0:T(8,128)(2,1)} custom-call(bf16[512,2560]{1,0:T(8,128)(2,1)} %pad_maximum_fusion.3.normed_ref.left_ref, bf16[512,1920]{1,0:T(8,128)(2,1)} %get-tuple-element.160.gate_ref.refs_0_, bf16[512,1920]{1,0:T(8,128)(2,1)} %get-tuple-element.151.lin_ref.refs_1_), custom_call_target="tpu_custom_call" | custom-call | flops 10066329600 | bytes 19660800 | tf_op jit(solution)/shard_map/pallas_call | solution.py:499
  375.7 9.5 %collective-permute-done.40 = bf16[128,1280]{1,0:T(8,128)(2,1)} collective-permute-done((bf16[128,1280]{1,0:T(8,128)(2,1)}, bf16[128,1280]{1,0:T(8,128)(2,1)}, u32[]{:S(2)}, u32[]{:S(2)}) %collective-permute-start.40) | collective-permute-done | bytes 327712 | tf_op jit(solution)/shard_map/ppermute | solution.py:62
  394.4 9.3 %collective-permute-done.43 = bf16[128,640]{1,0:T(8,128)(2,1)S(1)} collective-permute-done((bf16[128,640]{1,0:T(8,128)(2,1)S(1)}, bf16[128,640]{1,0:T(8,128)(2,1)S(1)}, u32[]{:S(2)}, u32[]{:S(2)}) %collective-permute-start.43) | collective-permute-done | bytes 163872 | tf_op jit(solution)/shard_map/ppermute | solution.py:62
  404.8 4.8 convolution_convert_fusion
  415.5 14.0 %collective-permute-done.47.refs_3_ = bf16[128,2560]{1,0:T(8,128)(2,1)S(1)} collective-permute-done((bf16[128,2560]{1,0:T(8,128)(2,1)S(1)}, bf16[128,2560]{1,0:T(8,128)(2,1)S(1)}, u32[]{:S(2)}, u32[]{:S(2)}) %collective-permute-start.47) | collective-permute-done | bytes 655392 | tf_op jit(solution)/shard_map/ppermute | solution.py:62
  429.5 24.9 %collective-permute-done.46.refs_2_ = bf16[128,2560]{1,0:T(8,128)(2,1)S(1)} collective-permute-done((bf16[128,2560]{1,0:T(8,128)(2,1)S(1)}, bf16[128,2560]{1,0:T(8,128)(2,1)S(1)}, u32[]{:S(2)}, u32[]{:S(2)}) %collective-permute-start.46) | collective-permute-done | bytes 655392 | tf_op jit(solution)/shard_map/ppermute | solution.py:62
  455.0 4.9 shard_map.467
  460.0 17.2 %collective-permute-start.50 = (bf16[128,768]{1,0:T(8,128)(2,1)S(1)}, bf16[128,768]{1,0:T(8,128)(2,1)S(1)}, u32[]{:S(2)}, u32[]{:S(2)}) collective-permute-start(bf16[128,768]{1,0:T(8,128)(2,1)S(1)} %get-tuple-element.262), channel_id=1, source_target_pairs={{0,3},{1,0},{2,1},{3,2},{4,7},{5,4},{6,5},{7,6},{8,11},{9,8},{10,9... | collective-permute-start | bytes 589832 | tf_op jit(solution)/shard_map/ppermute | solution.py:62
  478.2 4.5 collective-permute-done.50
  482.6 10.4 %collective-permute-done.49 = bf16[128,768]{1,0:T(8,128)(2,1)S(1)} collective-permute-done((bf16[128,768]{1,0:T(8,128)(2,1)S(1)}, bf16[128,768]{1,0:T(8,128)(2,1)S(1)}, u32[]{:S(2)}, u32[]{:S(2)}) %collective-permute-start.49) | collective-permute-done | bytes 196640 | tf_op jit(solution)/shard_map/ppermute | solution.py:62
  493.1 10.6 %shard_map.469 = (bf16[4,320,1408]{2,1,0:T(8,128)(2,1)}, bf16[4,320,1408]{2,1,0:T(8,128)(2,1)}) custom-call(s32[1]{0:T(128)} %bitcast.22.place_ref, bf16[512,2560]{1,0:T(8,128)(2,1)S(1)} %pad_maximum_fusion.2.left_a, bf16[512,640]{1,0:T(8,128)(2,1)S(1)} %pad_maximum_fusion.8.right_a, bf16[512,2560]{1,0:T(8,128)(2,1)} %fusion.2.left_b, ...), custom_call_target="tpu_custom_call" | custom-call | flops 3690987520 | bytes 7208960 | tf_op jit(solution)/shard_map/pallas_call | solution.py:284
  508.7 5.2 shard_map.468
  515.3 4.0 add_convert_fusion
  527.3 3.6 multiply_reduce_fusion
  532.2 9.1 %collective-permute-done.52 = bf16[2,320,640]{2,1,0:T(8,128)(2,1)} collective-permute-done((bf16[2,320,640]{2,1,0:T(8,128)(2,1)S(1)}, bf16[2,320,640]{2,1,0:T(8,128)(2,1)}, u32[]{:S(2)}, u32[]{:S(2)}) %collective-permute-start.52) | collective-permute-done | bytes 819232 | tf_op jit(solution)/shard_map/ppermute | solution.py:296
  544.0 3.5 collective-permute-done.54
  549.3 5.9 collective-permute-done.53
  571.5 3.3 collective-permute-done.59
  578.0 3.6 collective-permute-done.60
  583.6 28.1 %shard_map.470 = (f32[320,640]{1,0:T(8,128)}, f32[320,640]{1,0:T(8,128)}, f32[320,640]{1,0:T(8,128)}, f32[320,640]{1,0:T(8,128)}, bf16[320,640]{1,0:T(8,128)(2,1...) custom-call(f32[1,1]{1,0:T(1,128)} %bitcast.32.factor_ref, ...), custom_call_target="tpu_custom_call" | custom-call | bytes 68812800 | tf_op jit(solution)/shard_map/pallas_call | solution.py:552
  (349 shorter events, 132.9 us)
Async XLA Ops:
  7.2 82.8 %all-gather.3.cloned.1.call-start = ((), (), s32[]{:S(2)}) async-start(), calls=%async_computation.3 | async-start | bytes 8110080 | tf_op jit(solution)/shard_map/all_gather | solution.py:634
  10.6 233.1 %all-gather.5.cloned.1.call-start = ((), (), s32[]{:S(2)}) async-start(), calls=%async_computation.4 | async-start | bytes 33177600 | tf_op jit(solution)/shard_map/all_gather | solution.py:666
  11.4 13.5 %collective-permute-start.2 = (f32[8,128]{1,0:T(8,128)S(1)}, f32[8,128]{1,0:T(8,128)S(1)}, u32[]{:S(2)}, u32[]{:S(2)}) collective-permute-start(f32[8,128]{1,0:T(8,128)S(1)} %dynamic_update_slice.22), channel_id=1, source_target_pairs={{0,3},{1,0},{2,1},{3,2},{4,7},{5,4},{6,5},{7,6},{8,11},{9,8},{10,9... | collective-permute-start | bytes 12296 | tf_op jit(solution)/shard_map/ppermute | solution.py:62
  17.5 19.8 %collective-permute-start.6 = (bf16[128,2560]{1,0:T(8,128)(2,1)S(1)}, bf16[128,2560]{1,0:T(8,128)(2,1)}, u32[]{:S(2)}, u32[]{:S(2)}) collective-permute-start(bf16[128,2560]{1,0:T(8,128)(2,1)S(1)} %copy-done.6), channel_id=1, source_target_pairs={{0,1},{1,2},{2,3},{4,5},{5,6},{6,7},{8,9},{9,10},{10,11},{12,13},{... | collective-permute-start | bytes 1966088 | tf_op jit(solution)/shard_map/ppermute | solution.py:68
  22.7 17.3 %collective-permute-start.7 = (bf16[128,2560]{1,0:T(8,128)(2,1)S(1)}, bf16[128,2560]{1,0:T(8,128)(2,1)}, u32[]{:S(2)}, u32[]{:S(2)}) collective-permute-start(bf16[128,2560]{1,0:T(8,128)(2,1)S(1)} %copy-done.6), channel_id=1, source_target_pairs={{1,0},{2,1},{3,2},{5,4},{6,5},{7,6},{9,8},{10,9},{11,10},{13,12},{... | collective-permute-start | bytes 1966088 | tf_op jit(solution)/shard_map/ppermute | solution.py:69
  40.1 484.5 %reduce-scatter.6.cloned.1.call-start = ((), (), s32[]{:S(2)}) async-start(), calls=%async_computation.6 | async-start | bytes 11059200 | tf_op jit(solution)/shard_map/reduce_scatter | solution.py:720
  45.9 34.3 %collective-permute-start.9 = (bf16[128,2560]{1,0:T(8,128)(2,1)}, bf16[128,2560]{1,0:T(8,128)(2,1)S(1)}, u32[]{:S(2)}, u32[]{:S(2)}) collective-permute-start(bf16[128,2560]{1,0:T(8,128)(2,1)} %collective-permute-done.6), channel_id=1, source_target_pairs={{1,2},{2,3},{5,6},{6,7},{9,10},{10,11},{13,14},{14,15},{17,18},{18... | collective-permute-start | bytes 1966088 | tf_op jit(solution)/shard_map/ppermute | solution.py:80
  46.6 33.6 %collective-permute-start.10 = (bf16[128,2560]{1,0:T(8,128)(2,1)}, bf16[128,2560]{1,0:T(8,128)(2,1)S(1)}, u32[]{:S(2)}, u32[]{:S(2)}) collective-permute-start(bf16[128,2560]{1,0:T(8,128)(2,1)} %collective-permute-done.7), channel_id=1, source_target_pairs={{2,1},{1,0},{6,5},{5,4},{10,9},{9,8},{14,13},{13,12},{18,17},{17,1... | collective-permute-start | bytes 1966088 | tf_op jit(solution)/shard_map/ppermute | solution.py:82
  47.9 32.2 %collective-permute-start.8 = (bf16[128,2560]{1,0:T(8,128)(2,1)}, bf16[128,2560]{1,0:T(8,128)(2,1)S(1)}, u32[]{:S(2)}, u32[]{:S(2)}) collective-permute-start(bf16[128,2560]{1,0:T(8,128)(2,1)} %collective-permute-done.7), channel_id=1, source_target_pairs={{2,0},{6,4},{10,8},{14,12},{18,16},{22,20},{26,24},{30,28}} | collective-permute-start | bytes 1966088 | tf_op jit(solution)/shard_map/ppermute | solution.py:82
  80.5 21.3 %collective-permute-start.16 = (bf16[128,2560]{1,0:T(8,128)(2,1)}, bf16[128,2560]{1,0:T(8,128)(2,1)}, u32[]{:S(2)}, u32[]{:S(2)}) collective-permute-start(bf16[128,2560]{1,0:T(8,128)(2,1)} %fusion.19), channel_id=1, source_target_pairs={{1,0},{2,1},{3,2},{5,4},{6,5},{7,6},{9,8},{10,9},{11,10},{13,12},{... | collective-permute-start | bytes 1966088 | tf_op jit(solution)/shard_map/ppermute | solution.py:69
  81.8 20.0 %collective-permute-start.15 = (bf16[128,2560]{1,0:T(8,128)(2,1)}, bf16[128,2560]{1,0:T(8,128)(2,1)}, u32[]{:S(2)}, u32[]{:S(2)}) collective-permute-start(bf16[128,2560]{1,0:T(8,128)(2,1)} %fusion.19), channel_id=1, source_target_pairs={{0,1},{1,2},{2,3},{4,5},{5,6},{6,7},{8,9},{9,10},{10,11},{12,13},{... | collective-permute-start | bytes 1966088 | tf_op jit(solution)/shard_map/ppermute | solution.py:68
  98.0 14.5 %collective-permute-start.13 = (bf16[128,768]{1,0:T(8,128)(2,1)S(1)}, bf16[128,768]{1,0:T(8,128)(2,1)S(1)}, u32[]{:S(2)}, u32[]{:S(2)}) collective-permute-start(bf16[128,768]{1,0:T(8,128)(2,1)S(1)} %get-tuple-element.266), channel_id=1, source_target_pairs={{0,2},{1,3},{2,0},{3,1},{4,6},{5,7},{6,4},{7,5},{8,10},{9,11},{10,... | collective-permute-start | bytes 589832 | tf_op jit(solution)/shard_map/ppermute | solution.py:62
  98.8 13.6 %collective-permute-start.12 = (bf16[128,768]{1,0:T(8,128)(2,1)S(1)}, bf16[128,768]{1,0:T(8,128)(2,1)S(1)}, u32[]{:S(2)}, u32[]{:S(2)}) collective-permute-start(bf16[128,768]{1,0:T(8,128)(2,1)S(1)} %get-tuple-element.267), channel_id=1, source_target_pairs={{0,3},{1,0},{2,1},{3,2},{4,7},{5,4},{6,5},{7,6},{8,11},{9,8},{10,9... | collective-permute-start | bytes 589832 | tf_op jit(solution)/shard_map/ppermute | solution.py:62
  114.2 19.8 %collective-permute-start.18 = (bf16[128,2560]{1,0:T(8,128)(2,1)S(1)}, bf16[128,2560]{1,0:T(8,128)(2,1)S(1)}, u32[]{:S(2)}, u32[]{:S(2)}) collective-permute-start(bf16[128,2560]{1,0:T(8,128)(2,1)S(1)} %get-tuple-element.134), channel_id=1, source_target_pairs={{1,0},{2,1},{3,2},{5,4},{6,5},{7,6},{9,8},{10,9},{11,10},{13,12},{... | collective-permute-start | bytes 1966088 | tf_op jit(solution)/shard_map/ppermute | solution.py:69
  115.5 21.1 %collective-permute-start.17 = (bf16[128,2560]{1,0:T(8,128)(2,1)S(1)}, bf16[128,2560]{1,0:T(8,128)(2,1)S(1)}, u32[]{:S(2)}, u32[]{:S(2)}) collective-permute-start(bf16[128,2560]{1,0:T(8,128)(2,1)S(1)} %get-tuple-element.134), channel_id=1, source_target_pairs={{0,1},{1,2},{2,3},{4,5},{5,6},{6,7},{8,9},{9,10},{10,11},{12,13},{... | collective-permute-start | bytes 1966088 | tf_op jit(solution)/shard_map/ppermute | solution.py:68
  134.1 20.5 %collective-permute-start.19 = (bf16[128,2560]{1,0:T(8,128)(2,1)S(1)}, bf16[128,2560]{1,0:T(8,128)(2,1)S(1)}, u32[]{:S(2)}, u32[]{:S(2)}) collective-permute-start(bf16[128,2560]{1,0:T(8,128)(2,1)S(1)} %collective-permute-done.18), channel_id=1, source_target_pairs={{2,0},{6,4},{10,8},{14,12},{18,16},{22,20},{26,24},{30,28}} | collective-permute-start | bytes 1966088 | tf_op jit(solution)/shard_map/ppermute | solution.py:82
  135.4 30.9 %collective-permute-start.21 = (bf16[128,2560]{1,0:T(8,128)(2,1)S(1)}, bf16[128,2560]{1,0:T(8,128)(2,1)S(1)}, u32[]{:S(2)}, u32[]{:S(2)}) collective-permute-start(bf16[128,2560]{1,0:T(8,128)(2,1)S(1)} %collective-permute-done.18), channel_id=1, source_target_pairs={{2,1},{1,0},{6,5},{5,4},{10,9},{9,8},{14,13},{13,12},{18,17},{17,1... | collective-permute-start | bytes 1966088 | tf_op jit(solution)/shard_map/ppermute | solution.py:82
  136.7 17.9 %collective-permute-start.22 = (bf16[128,2560]{1,0:T(8,128)(2,1)S(1)}, bf16[128,2560]{1,0:T(8,128)(2,1)S(1)}, u32[]{:S(2)}, u32[]{:S(2)}) collective-permute-start(bf16[128,2560]{1,0:T(8,128)(2,1)S(1)} %collective-permute-done.17), channel_id=1, source_target_pairs={{1,3},{5,7},{9,11},{13,15},{17,19},{21,23},{25,27},{29,31}} | collective-permute-start | bytes 1966088 | tf_op jit(solution)/shard_map/ppermute | solution.py:80
  137.4 28.9 %collective-permute-start.20 = (bf16[128,2560]{1,0:T(8,128)(2,1)S(1)}, bf16[128,2560]{1,0:T(8,128)(2,1)S(1)}, u32[]{:S(2)}, u32[]{:S(2)}) collective-permute-start(bf16[128,2560]{1,0:T(8,128)(2,1)S(1)} %collective-permute-done.17), channel_id=1, source_target_pairs={{1,2},{2,3},{5,6},{6,7},{9,10},{10,11},{13,14},{14,15},{17,18},{18... | collective-permute-start | bytes 1966088 | tf_op jit(solution)/shard_map/ppermute | solution.py:80
  176.1 13.7 %collective-permute-start.24 = (bf16[128,640]{1,0:T(8,128)(2,1)}, bf16[128,640]{1,0:T(8,128)(2,1)}, u32[]{:S(2)}, u32[]{:S(2)}) collective-permute-start(bf16[128,640]{1,0:T(8,128)(2,1)} %get-tuple-element.274), channel_id=1, source_target_pairs={{0,2},{1,3},{2,0},{3,1},{4,6},{5,7},{6,4},{7,5},{8,10},{9,11},{10,... | collective-permute-start | bytes 491528 | tf_op jit(solution)/shard_map/ppermute | solution.py:62
  176.1 13.7 %collective-permute-start.23 = (bf16[128,640]{1,0:T(8,128)(2,1)}, bf16[128,640]{1,0:T(8,128)(2,1)}, u32[]{:S(2)}, u32[]{:S(2)}) collective-permute-start(bf16[128,640]{1,0:T(8,128)(2,1)} %get-tuple-element.275), channel_id=1, source_target_pairs={{0,1},{1,2},{2,3},{3,0},{4,5},{5,6},{6,7},{7,4},{8,9},{9,10},{10,1... | collective-permute-start | bytes 491528 | tf_op jit(solution)/shard_map/ppermute | solution.py:62
  192.1 17.9 %collective-permute-start.27 = (bf16[128,2560]{1,0:T(8,128)(2,1)S(1)}, bf16[128,2560]{1,0:T(8,128)(2,1)S(1)}, u32[]{:S(2)}, u32[]{:S(2)}) collective-permute-start(bf16[128,2560]{1,0:T(8,128)(2,1)S(1)} %multiply_convert_fusion.1), channel_id=1, source_target_pairs={{1,0},{2,1},{3,2},{5,4},{6,5},{7,6},{9,8},{10,9},{11,10},{13,12},{... | collective-permute-start | bytes 1966088 | tf_op jit(solution)/shard_map/ppermute | solution.py:69
  193.4 19.2 %collective-permute-start.26 = (bf16[128,2560]{1,0:T(8,128)(2,1)S(1)}, bf16[128,2560]{1,0:T(8,128)(2,1)S(1)}, u32[]{:S(2)}, u32[]{:S(2)}) collective-permute-start(bf16[128,2560]{1,0:T(8,128)(2,1)S(1)} %multiply_convert_fusion.1), channel_id=1, source_target_pairs={{0,1},{1,2},{2,3},{4,5},{5,6},{6,7},{8,9},{9,10},{10,11},{12,13},{... | collective-permute-start | bytes 1966088 | tf_op jit(solution)/shard_map/ppermute | solution.py:68
  210.0 20.4 %collective-permute-start.28 = (bf16[128,2560]{1,0:T(8,128)(2,1)S(1)}, bf16[128,2560]{1,0:T(8,128)(2,1)S(1)}, u32[]{:S(2)}, u32[]{:S(2)}) collective-permute-start(bf16[128,2560]{1,0:T(8,128)(2,1)S(1)} %collective-permute-done.27), channel_id=1, source_target_pairs={{2,0},{6,4},{10,8},{14,12},{18,16},{22,20},{26,24},{30,28}} | collective-permute-start | bytes 1966088 | tf_op jit(solution)/shard_map/ppermute | solution.py:82
  211.3 30.6 %collective-permute-start.30 = (bf16[128,2560]{1,0:T(8,128)(2,1)S(1)}, bf16[128,2560]{1,0:T(8,128)(2,1)S(1)}, u32[]{:S(2)}, u32[]{:S(2)}) collective-permute-start(bf16[128,2560]{1,0:T(8,128)(2,1)S(1)} %collective-permute-done.27), channel_id=1, source_target_pairs={{2,1},{1,0},{6,5},{5,4},{10,9},{9,8},{14,13},{13,12},{18,17},{17,1... | collective-permute-start | bytes 1966088 | tf_op jit(solution)/shard_map/ppermute | solution.py:82
  212.6 17.9 %collective-permute-start.31 = (bf16[128,2560]{1,0:T(8,128)(2,1)S(1)}, bf16[128,2560]{1,0:T(8,128)(2,1)S(1)}, u32[]{:S(2)}, u32[]{:S(2)}) collective-permute-start(bf16[128,2560]{1,0:T(8,128)(2,1)S(1)} %collective-permute-done.26), channel_id=1, source_target_pairs={{1,3},{5,7},{9,11},{13,15},{17,19},{21,23},{25,27},{29,31}} | collective-permute-start | bytes 1966088 | tf_op jit(solution)/shard_map/ppermute | solution.py:80
  213.3 28.6 %collective-permute-start.29 = (bf16[128,2560]{1,0:T(8,128)(2,1)S(1)}, bf16[128,2560]{1,0:T(8,128)(2,1)S(1)}, u32[]{:S(2)}, u32[]{:S(2)}) collective-permute-start(bf16[128,2560]{1,0:T(8,128)(2,1)S(1)} %collective-permute-done.26), channel_id=1, source_target_pairs={{1,2},{2,3},{5,6},{6,7},{9,10},{10,11},{13,14},{14,15},{17,18},{18... | collective-permute-start | bytes 1966088 | tf_op jit(solution)/shard_map/ppermute | solution.py:80
  243.6 32.8 %collective-permute-start.35 = (bf16[128,2560]{1,0:T(8,128)(2,1)}, bf16[128,2560]{1,0:T(8,128)(2,1)S(1)}, u32[]{:S(2)}, u32[]{:S(2)}) collective-permute-start(bf16[128,2560]{1,0:T(8,128)(2,1)} %collective-permute-done.15), channel_id=1, source_target_pairs={{1,3},{5,7},{9,11},{13,15},{17,19},{21,23},{25,27},{29,31}} | collective-permute-start | bytes 1966088 | tf_op jit(solution)/shard_map/ppermute | solution.py:80
  244.3 40.5 %collective-permute-start.33 = (bf16[128,2560]{1,0:T(8,128)(2,1)}, bf16[128,2560]{1,0:T(8,128)(2,1)S(1)}, u32[]{:S(2)}, u32[]{:S(2)}) collective-permute-start(bf16[128,2560]{1,0:T(8,128)(2,1)} %collective-permute-done.15), channel_id=1, source_target_pairs={{1,2},{2,3},{5,6},{6,7},{9,10},{10,11},{13,14},{14,15},{17,18},{18... | collective-permute-start | bytes 1966088 | tf_op jit(solution)/shard_map/ppermute | solution.py:80
  245.1 39.8 %collective-permute-start.34 = (bf16[128,2560]{1,0:T(8,128)(2,1)}, bf16[128,2560]{1,0:T(8,128)(2,1)S(1)}, u32[]{:S(2)}, u32[]{:S(2)}) collective-permute-start(bf16[128,2560]{1,0:T(8,128)(2,1)} %collective-permute-done.16), channel_id=1, source_target_pairs={{2,1},{1,0},{6,5},{5,4},{10,9},{9,8},{14,13},{13,12},{18,17},{17,1... | collective-permute-start | bytes 1966088 | tf_op jit(solution)/shard_map/ppermute | solution.py:82
  246.4 38.4 %collective-permute-start.32 = (bf16[128,2560]{1,0:T(8,128)(2,1)}, bf16[128,2560]{1,0:T(8,128)(2,1)S(1)}, u32[]{:S(2)}, u32[]{:S(2)}) collective-permute-start(bf16[128,2560]{1,0:T(8,128)(2,1)} %collective-permute-done.16), channel_id=1, source_target_pairs={{2,0},{6,4},{10,8},{14,12},{18,16},{22,20},{26,24},{30,28}} | collective-permute-start | bytes 1966088 | tf_op jit(solution)/shard_map/ppermute | solution.py:82
  297.0 230.3 %reduce-scatter.8.cloned.1.call-start = ((), (), s32[]{:S(2)}) async-start(), calls=%async_computation.7 | async-start | bytes 22118400 | tf_op jit(solution)/shard_map/reduce_scatter | solution.py:729
  324.4 19.1 %collective-permute-start.36 = (bf16[128,1280]{1,0:T(8,128)(2,1)}, bf16[128,1280]{1,0:T(8,128)(2,1)}, u32[]{:S(2)}, u32[]{:S(2)}) collective-permute-start(bf16[128,1280]{1,0:T(8,128)(2,1)} %get-tuple-element.153), channel_id=1, source_target_pairs={{0,3},{1,0},{2,1},{3,2},{4,7},{5,4},{6,5},{7,6},{8,11},{9,8},{10,9... | collective-permute-start | bytes 983048 | tf_op jit(solution)/shard_map/ppermute | solution.py:62
  324.4 34.9 %collective-permute-start.37 = (bf16[128,1280]{1,0:T(8,128)(2,1)}, bf16[128,1280]{1,0:T(8,128)(2,1)}, u32[]{:S(2)}, u32[]{:S(2)}) collective-permute-start(bf16[128,1280]{1,0:T(8,128)(2,1)} %get-tuple-element.154), channel_id=1, source_target_pairs={{0,2},{1,3},{2,0},{3,1},{4,6},{5,7},{6,4},{7,5},{8,10},{9,11},{10,... | collective-permute-start | bytes 983048 | tf_op jit(solution)/shard_map/ppermute | solution.py:62
  328.2 31.1 %collective-permute-start.38 = (bf16[128,1280]{1,0:T(8,128)(2,1)}, bf16[128,1280]{1,0:T(8,128)(2,1)}, u32[]{:S(2)}, u32[]{:S(2)}) collective-permute-start(bf16[128,1280]{1,0:T(8,128)(2,1)} %get-tuple-element.155), channel_id=1, source_target_pairs={{0,1},{1,2},{2,3},{3,0},{4,5},{5,6},{6,7},{7,4},{8,9},{9,10},{10,1... | collective-permute-start | bytes 983048 | tf_op jit(solution)/shard_map/ppermute | solution.py:62
  341.7 34.0 %collective-permute-start.39 = (bf16[128,1280]{1,0:T(8,128)(2,1)}, bf16[128,1280]{1,0:T(8,128)(2,1)}, u32[]{:S(2)}, u32[]{:S(2)}) collective-permute-start(bf16[128,1280]{1,0:T(8,128)(2,1)} %get-tuple-element.162), channel_id=1, source_target_pairs={{0,3},{1,0},{2,1},{3,2},{4,7},{5,4},{6,5},{7,6},{8,11},{9,8},{10,9... | collective-permute-start | bytes 983048 | tf_op jit(solution)/shard_map/ppermute | solution.py:62
  343.5 41.6 %collective-permute-start.40 = (bf16[128,1280]{1,0:T(8,128)(2,1)}, bf16[128,1280]{1,0:T(8,128)(2,1)}, u32[]{:S(2)}, u32[]{:S(2)}) collective-permute-start(bf16[128,1280]{1,0:T(8,128)(2,1)} %get-tuple-element.163), channel_id=1, source_target_pairs={{0,2},{1,3},{2,0},{3,1},{4,6},{5,7},{6,4},{7,5},{8,10},{9,11},{10,... | collective-permute-start | bytes 983048 | tf_op jit(solution)/shard_map/ppermute | solution.py:62
  343.5 41.6 %collective-permute-start.41 = (bf16[128,1280]{1,0:T(8,128)(2,1)}, bf16[128,1280]{1,0:T(8,128)(2,1)}, u32[]{:S(2)}, u32[]{:S(2)}) collective-permute-start(bf16[128,1280]{1,0:T(8,128)(2,1)} %get-tuple-element.164), channel_id=1, source_target_pairs={{0,1},{1,2},{2,3},{3,0},{4,5},{5,6},{6,7},{7,4},{8,9},{9,10},{10,1... | collective-permute-start | bytes 983048 | tf_op jit(solution)/shard_map/ppermute | solution.py:62
  385.2 227.8 %reduce-scatter.4.cloned.1.call-start = ((), (), s32[]{:S(2)}) async-start(), calls=%async_computation.5 | async-start | bytes 6553600 | tf_op jit(solution)/shard_map/reduce_scatter | solution.py:771
  409.9 19.7 %collective-permute-start.47 = (bf16[128,2560]{1,0:T(8,128)(2,1)S(1)}, bf16[128,2560]{1,0:T(8,128)(2,1)S(1)}, u32[]{:S(2)}, u32[]{:S(2)}) collective-permute-start(bf16[128,2560]{1,0:T(8,128)(2,1)S(1)} %get-tuple-element.235), channel_id=1, source_target_pairs={{0,1},{1,2},{2,3},{3,0},{4,5},{5,6},{6,7},{7,4},{8,9},{9,10},{10,1... | collective-permute-start | bytes 1966088 | tf_op jit(solution)/shard_map/ppermute | solution.py:62
  412.9 41.5 %collective-permute-start.46 = (bf16[128,2560]{1,0:T(8,128)(2,1)S(1)}, bf16[128,2560]{1,0:T(8,128)(2,1)S(1)}, u32[]{:S(2)}, u32[]{:S(2)}) collective-permute-start(bf16[128,2560]{1,0:T(8,128)(2,1)S(1)} %get-tuple-element.236), channel_id=1, source_target_pairs={{0,2},{1,3},{2,0},{3,1},{4,6},{5,7},{6,4},{7,5},{8,10},{9,11},{10,... | collective-permute-start | bytes 1966088 | tf_op jit(solution)/shard_map/ppermute | solution.py:62
  412.9 42.1 %collective-permute-start.45 = (bf16[128,2560]{1,0:T(8,128)(2,1)S(1)}, bf16[128,2560]{1,0:T(8,128)(2,1)S(1)}, u32[]{:S(2)}, u32[]{:S(2)}) collective-permute-start(bf16[128,2560]{1,0:T(8,128)(2,1)S(1)} %get-tuple-element.237), channel_id=1, source_target_pairs={{0,3},{1,0},{2,1},{3,2},{4,7},{5,4},{6,5},{7,6},{8,11},{9,8},{10,9... | collective-permute-start | bytes 1966088 | tf_op jit(solution)/shard_map/ppermute | solution.py:62
  460.0 22.6 %collective-permute-start.50 = (bf16[128,768]{1,0:T(8,128)(2,1)S(1)}, bf16[128,768]{1,0:T(8,128)(2,1)S(1)}, u32[]{:S(2)}, u32[]{:S(2)}) collective-permute-start(bf16[128,768]{1,0:T(8,128)(2,1)S(1)} %get-tuple-element.262), channel_id=1, source_target_pairs={{0,3},{1,0},{2,1},{3,2},{4,7},{5,4},{6,5},{7,6},{8,11},{9,8},{10,9... | collective-permute-start | bytes 589832 | tf_op jit(solution)/shard_map/ppermute | solution.py:62
  477.2 15.8 %collective-permute-start.49 = (bf16[128,768]{1,0:T(8,128)(2,1)S(1)}, bf16[128,768]{1,0:T(8,128)(2,1)S(1)}, u32[]{:S(2)}, u32[]{:S(2)}) collective-permute-start(bf16[128,768]{1,0:T(8,128)(2,1)S(1)} %get-tuple-element.263), channel_id=1, source_target_pairs={{0,2},{1,3},{2,0},{3,1},{4,6},{5,7},{6,4},{7,5},{8,10},{9,11},{10,... | collective-permute-start | bytes 589832 | tf_op jit(solution)/shard_map/ppermute | solution.py:62
  477.2 15.8 %collective-permute-start.48 = (bf16[128,768]{1,0:T(8,128)(2,1)S(1)}, bf16[128,768]{1,0:T(8,128)(2,1)S(1)}, u32[]{:S(2)}, u32[]{:S(2)}) collective-permute-start(bf16[128,768]{1,0:T(8,128)(2,1)S(1)} %get-tuple-element.264), channel_id=1, source_target_pairs={{0,1},{1,2},{2,3},{3,0},{4,5},{5,6},{6,7},{7,4},{8,9},{9,10},{10,1... | collective-permute-start | bytes 589832 | tf_op jit(solution)/shard_map/ppermute | solution.py:62
  520.6 20.6 %collective-permute-start.52 = (bf16[2,320,640]{2,1,0:T(8,128)(2,1)S(1)}, bf16[2,320,640]{2,1,0:T(8,128)(2,1)}, u32[]{:S(2)}, u32[]{:S(2)}) collective-permute-start(bf16[2,320,640]{2,1,0:T(8,128)(2,1)S(1)} %get-tuple-element.244), channel_id=1, source_target_pairs={{0,8},{4,12},{8,0},{12,4},{16,24},{20,28},{24,16},{28,20},{1,9},{5... | collective-permute-start | bytes 2457608 | tf_op jit(solution)/shard_map/ppermute | solution.py:296
  522.6 25.0 %collective-permute-start.54 = (bf16[2,320,768]{2,1,0:T(8,128)(2,1)}, bf16[2,320,768]{2,1,0:T(8,128)(2,1)}, u32[]{:S(2)}, u32[]{:S(2)}) collective-permute-start(bf16[2,320,768]{2,1,0:T(8,128)(2,1)} %get-tuple-element.233), channel_id=1, source_target_pairs={{0,16},{4,20},{8,24},{12,28},{16,0},{20,4},{24,8},{28,12},{1,17},{... | collective-permute-start | bytes 2949128 | tf_op jit(solution)/shard_map/ppermute | solution.py:296
  522.7 26.5 %collective-permute-start.62 = (f32[4,2560]{1,0:T(4,128)S(1)}, f32[4,2560]{1,0:T(4,128)S(1)}, u32[]{:S(2)}, u32[]{:S(2)}) collective-permute-start(f32[4,2560]{1,0:T(4,128)S(1)} %fusion.63), channel_id=1, source_target_pairs={{0,2},{1,3},{2,0},{3,1},{4,6},{5,7},{6,4},{7,5},{8,10},{9,11},{10,... | collective-permute-start | bytes 122888 | tf_op jit(solution)/shard_map/ppermute | solution.py:570
  (77 other events, 1028.9 us)
Sparse Core Ops, SparseCore 0:
  10.7 52.4 all-gather.2
  65.7 143.6 all-gather.4
  297.1 79.0 reduce-scatter.5
  385.3 130.5 reduce-scatter.7
  518.1 94.8 reduce-scatter.3
